TPU v7x, 32 devices: a whole 2x2x4 slice. The times are simulated.
32 devices in a mesh: expert: 8 (over z, x), replica: 4 (over y, core).
Axes of the slice: x: 2, y: 2, z: 4, core: 2. Of those that a mesh axis runs over, the one named last changes fastest.
Arguments:
- grad_out: bfloat16 [4096, 2048], P(('expert', 'replica')), may hold values from -6 to 6
- gates: bfloat16 [4096, 8], P(('expert', 'replica')), may hold values from 0.019897461 to 0.5
- experts: int32 [4096, 8], P(('expert', 'replica')), may hold values from 0 to 31, all different within a row; in each aligned block of 128 rows (0 to 127, 128 to 255, ...) at most 80 rows name the same one
- hidden: bfloat16 [32, 4, 640, 768], P('expert', 'replica'), may hold values from -6 to 6
- down_weight: bfloat16 [2048, 32, 768], P(None, 'expert'), may hold values from -0.21875 to 0.21875
Outputs:
- d_hidden: bfloat16 [32, 4, 640, 768], P('expert', 'replica')
- d_down: bfloat16 [2048, 32, 768], P('replica', 'expert')
- d_gates: float32 [4096, 8], P(('expert', 'replica'))
Inputs may be any that keep to these rules, and one draw needn't show every extreme that they name: Each token names 8 different experts. Among the 128 tokens of one device no expert is named by more than 80 tokens, a bound that some block reaches.
All inputs are finite; a program needn't handle non-finite values.
Results may differ from a plain program's by a relative error of at most 0.013.
Values may be sent and summed in bfloat16 or wider, within the bound.
No kernel may reach another device: no remote copies, remote signals or barrier semaphores. Data moves between devices by JAX's collectives and lax.ppermute only.
A program may use at most 192 MiB of HBM per device.

v0:
```python
import jax
import jax.numpy as jnp
from jax import lax
from jax.sharding import PartitionSpec as P


def per_device(grad_out, gates, experts, hidden, down_weight):
    expert_count = lax.axis_size("expert")
    tok_rows = grad_out.shape[0]
    top_count = experts.shape[1]
    local_experts = hidden.shape[0]
    slot_count = hidden.shape[2]
    hidden_width = hidden.shape[3]
    capacity = slot_count // expert_count
    all_experts = local_experts * expert_count
    flat_ids = experts.reshape(-1)
    expert_range = jnp.arange(all_experts, dtype=jnp.int32)
    onehot_ids = (flat_ids[:, None] == expert_range[None, :]).astype(jnp.int32)
    running = jnp.cumsum(onehot_ids, axis=0)
    position = jnp.sum(onehot_ids * running, axis=1) - 1
    slot_index = (
        flat_ids % local_experts * expert_count + flat_ids // local_experts
    ) * capacity + position
    slot_index = slot_index.reshape(tok_rows, top_count)
    slot_range = jnp.arange(all_experts * capacity, dtype=jnp.int32)
    matches = slot_index[:, :, None] == slot_range[None, None, :]
    placing = jnp.any(matches, axis=1).astype(jnp.bfloat16)
    outgoing = jnp.einsum(
        "tr,td->rd", placing, grad_out, preferred_element_type=jnp.float32
    ).astype(jnp.bfloat16)
    out_gates = jnp.sum(
        jnp.where(matches, gates[:, :, None].astype(jnp.float32), 0.0), axis=(0, 1)
    ).astype(jnp.bfloat16)
    outgoing = outgoing.reshape(local_experts, expert_count, capacity, outgoing.shape[1])
    out_gates = out_gates.reshape(local_experts, expert_count, capacity)
    grad_slots, gate_slots = (
        lax.all_to_all(outgoing, "expert", split_axis=1, concat_axis=1, tiled=True),
        lax.all_to_all(out_gates, "expert", split_axis=1, concat_axis=1, tiled=True),
    )
    grad_slots = grad_slots.reshape(local_experts, slot_count, grad_slots.shape[3])
    gate_slots = gate_slots.reshape(local_experts, slot_count).astype(jnp.float32)
    hidden_slots = hidden.reshape(local_experts, slot_count, hidden_width)
    upstream = jnp.einsum(
        "esd,def->esf", grad_slots, down_weight, preferred_element_type=jnp.float32
    )
    hidden_grad = (gate_slots[:, :, None] * upstream).astype(jnp.bfloat16).reshape(hidden.shape)
    slot_grad = jnp.sum(hidden_slots.astype(jnp.float32) * upstream, axis=2)
    weighted = (gate_slots[:, :, None] * hidden_slots.astype(jnp.float32)).astype(jnp.bfloat16)
    down_grad = lax.psum_scatter(
        jnp.einsum("esd,esf->def", grad_slots, weighted, preferred_element_type=jnp.float32).astype(
            jnp.bfloat16
        ),
        "replica",
        scatter_dimension=0,
        tiled=True,
    )
    returned = lax.all_to_all(
        slot_grad.reshape(local_experts, expert_count, capacity),
        "expert",
        split_axis=1,
        concat_axis=1,
        tiled=True,
    )
    gate_grad = jnp.take(returned.reshape(-1), slot_index, axis=0)
    return (hidden_grad, down_grad, gate_grad)


def solution(mesh):
    in_specs = (
        P(("expert", "replica"), None),
        P(("expert", "replica"), None),
        P(("expert", "replica"), None),
        P("expert", "replica", None, None),
        P(None, "expert", None),
    )
    out_specs = (
        P("expert", "replica", None, None),
        P("replica", "expert", None),
        P(("expert", "replica"), None),
    )
    return jax.shard_map(
        per_device, mesh=mesh, in_specs=in_specs, out_specs=out_specs, check_vma=False
    )
```

profile of v0, /device:TPU:0, one launch (start us, length us, event | category | flops | bytes accessed | tf_op | source)
XLA Modules:
  0.0 420.4 jit_solution(14401564991402892614)
XLA Ops:
  7.2 0.0 copy-start
  7.2 0.8 copy.89
  8.0 0.1 eq.40
  8.1 0.1 eq.44
  8.2 0.8 copy.97
  9.0 9.0 %reduce-window.6 = s32[32,8,128]{2,1,0:T(8,128)S(1)} reduce-window(s32[32,8,128]{2,1,0:T(8,128)S(1)} %fusion.11, s32[]{:T(128)} %constant.47.clone.1), window={size=1x1x128 pad=0_0x0_0x127_0}, to_apply=%region_0.0 | reduce-window | flops 4161536 | bytes 262148 | tf_op jit(solution)/shard_map/reduce-window
  18.0 0.1 slice.10
  18.1 0.1 copy.95
  18.3 0.1 copy.96
  18.4 0.1 broadcast_add_fusion
  18.5 0.1 sub.14
  18.6 0.1 compare_select_fusion
  18.7 1.6 select_reduce_fusion
  20.3 0.1 convert_element_type.52
  20.4 0.6 copy.98
  21.0 7.3 %all-to-all-start = ((bf16[4,8,80]{2,0,1:T(4,128)(2,1)}), bf16[4,8,80]{2,0,1:T(4,128)(2,1)S(1)}, u32[]{:S(2)}, u32[]{:S(2)}) async-start(bf16[4,8,80]{2,0,1:T(4,128)(2,1)} %copy.98), calls=%async_computation | async-start | bytes 16384 | tf_op jit(solution)/shard_map/all_to_all | solution.py:38
  28.2 5.0 %fusion.2 = pred[128,2560]{1,0:T(8,128)(4,1)S(1)} fusion(s32[128,8]{1,0:T(8,128)S(1)} %get-tuple-element.22), kind=kLoop, calls=%fused_computation.7 | loop fusion | flops 4915200 | bytes 331776 | tf_op jit(solution)/shard_map/reduce_or | solution.py:27
  33.2 0.0 copy-done
  33.2 5.6 %convolution_convert_fusion = bf16[2560,2048]{1,0:T(8,128)(2,1)} fusion(pred[128,2560]{1,0:T(8,128)(4,1)S(1)} %fusion.2, bf16[128,2048]{1,0:T(8,128)(2,1)S(1)} %copy-done), kind=kOutput, calls=%fused_computation.4 | convolution fusion | flops 1347420160 | bytes 11337728 | tf_op jit(solution)/shard_map/tr,td->rd/dot_general | solution.py:28
  38.8 10.0 %copy.100 = bf16[4,8,80,2048]{3,2,0,1:T(8,128)(2,1)} copy(bf16[4,8,80,2048]{3,2,1,0:T(8,128)(2,1)} %bitcast.35) | data formatting | bytes 20971520 | tf_op jit(solution)/shard_map/reshape | solution.py:34
  48.8 0.0 all-to-all-done
  48.8 6.0 %all-to-all-start.1 = ((bf16[4,8,80,2048]{3,2,0,1:T(8,128)(2,1)}), bf16[4,8,80,2048]{3,2,0,1:T(8,128)(2,1)}, u32[]{:S(2)}, u32[]{:S(2)}) async-start(bf16[4,8,80,2048]{3,2,0,1:T(8,128)(2,1)} %copy.100), calls=%async_computation.1 | async-start | bytes 20971520 | tf_op jit(solution)/shard_map/all_to_all | solution.py:37
  54.8 0.2 reduce-scatter.2.cloned.1.call-start
  55.1 0.1 reshape.105
  55.2 227.2 %all-to-all-done.1 = bf16[4,8,80,2048]{3,2,0,1:T(8,128)(2,1)} async-done(((bf16[4,8,80,2048]{3,2,0,1:T(8,128)(2,1)}), bf16[4,8,80,2048]{3,2,0,1:T(8,128)(2,1)}, u32[]{:S(2)}, u32[]{:S(2)}) %all-to-all-start.1) | async-done | bytes 10485792 | tf_op jit(solution)/shard_map/all_to_all | solution.py:37
  282.4 10.1 %copy.101 = bf16[4,8,80,2048]{3,2,1,0:T(8,128)(2,1)} copy(bf16[4,8,80,2048]{3,2,0,1:T(8,128)(2,1)} %all-to-all-done.1) | data formatting | bytes 20971520 | tf_op jit(solution)/shard_map/all_to_all | solution.py:37
  292.5 16.8 %convert_bitcast_fusion = bf16[2048,4,768]{0,2,1:T(8,128)(2,1)} fusion(bf16[4,640,2048]{2,1,0:T(8,128)(2,1)} %bitcast.36, bf16[4,1,640,768]{3,2,1,0:T(8,128)(2,1)} %param.8, f32[4,640]{1,0:T(4,128)S(1)} %reshape.105), kind=kOutput, calls=%fused_computation.3 | convolution fusion | flops 8065253376 | bytes 27011072 | tf_op jit(solution)/shard_map/esd,esf->def/dot_general | solution.py:50
  309.3 0.0 reduce-scatter.2.cloned.1.call-update
  309.3 0.1 reshape.109
  309.4 20.4 %fusion.4 = (f32[4,640]{1,0:T(4,128)S(1)}, bf16[4,1,640,768]{3,2,1,0:T(8,128)(2,1)}) fusion(bf16[4,1,640,768]{3,2,1,0:T(8,128)(2,1)} %param.8, f32[4,640]{1,0:T(4,128)S(1)} %reshape.105, bf16[4,640,2048]{2,1,0:T(8,128)(2,1)} %bitcast.37, bf16[2048,4,768]{2,1,0:T(4,128)(2,1)} %param.9), kind=kOutput, calls=%fused_computation.11 | convolution fusion | flops 8062891520 | bytes 30953472 | tf_op jit(solution)/shard_map/esd,def->esf/dot_general | solution.py:43
  329.7 0.1 reshape.103
  329.8 0.6 copy.105
  330.4 3.3 all-to-all-start.2
  333.8 6.5 %all-to-all-done.2 = f32[4,8,80]{2,0,1:T(4,128)S(1)} async-done(((f32[4,8,80]{2,0,1:T(4,128)}), f32[4,8,80]{2,0,1:T(4,128)S(1)}, u32[]{:S(2)}, u32[]{:S(2)}) %all-to-all-start.2) | async-done | bytes 10272 | tf_op jit(solution)/shard_map/all_to_all | solution.py:57
  340.3 0.1 reshape.104
  340.4 0.0 copy-start.1
  340.4 6.1 %gather_fusion = f32[1024]{0:T(1024)S(1)} fusion(f32[2560]{0:T(1024)S(1)} %reshape.104, s32[1024]{0:T(1024)S(1)} %broadcast_clamp_fusion), kind=kCustom, calls=%fused_computation | custom fusion | bytes 12288 | tf_op jit(solution)/shard_map/jit(_take)/gather | solution.py:64
  346.5 0.1 reshape.108
  346.6 0.7 copy.109
  347.3 60.3 %reduce-scatter.2.cloned.1.call-done = bf16[512,4,768]{0,2,1:T(8,128)(2,1)} async-done(((bf16[2048,4,768]{0,2,1:T(8,128)(2,1)}), bf16[512,4,768]{0,2,1:T(8,128)(2,1)}) %reduce-scatter.2.cloned.1.call-update) | async-done | bytes 3145744 | tf_op jit(solution)/shard_map/reduce_scatter | solution.py:49
  407.6 6.0 %copy.108 = bf16[512,4,768]{2,1,0:T(4,128)(2,1)} copy(bf16[512,4,768]{0,2,1:T(8,128)(2,1)} %reduce-scatter.2.cloned.1.call-done) | data formatting | bytes 6291456
  413.5 0.0 copy-done.1
  (9 shorter events, 0.1 us)
Async XLA Ops:
  7.2 26.1 %copy-start = (bf16[128,2048]{1,0:T(8,128)(2,1)S(1)}, bf16[128,2048]{1,0:T(8,128)(2,1)}, u32[]{:S(2)}) copy-start(bf16[128,2048]{1,0:T(8,128)(2,1)} %param.5) | copy-start | bytes 1572868
  21.0 27.9 %all-to-all-start = ((bf16[4,8,80]{2,0,1:T(4,128)(2,1)}), bf16[4,8,80]{2,0,1:T(4,128)(2,1)S(1)}, u32[]{:S(2)}, u32[]{:S(2)}) async-start(bf16[4,8,80]{2,0,1:T(4,128)(2,1)} %copy.98), calls=%async_computation | async-start | bytes 16384 | tf_op jit(solution)/shard_map/all_to_all | solution.py:38
  48.8 233.5 %all-to-all-start.1 = ((bf16[4,8,80,2048]{3,2,0,1:T(8,128)(2,1)}), bf16[4,8,80,2048]{3,2,0,1:T(8,128)(2,1)}, u32[]{:S(2)}, u32[]{:S(2)}) async-start(bf16[4,8,80,2048]{3,2,0,1:T(8,128)(2,1)} %copy.100), calls=%async_computation.1 | async-start | bytes 20971520 | tf_op jit(solution)/shard_map/all_to_all | solution.py:37
  54.8 352.7 %reduce-scatter.2.cloned.1.call-start = ((), (), s32[]{:S(2)}) async-start(), calls=%async_computation.4 | async-start | bytes 15728640 | tf_op jit(solution)/shard_map/reduce_scatter | solution.py:49
  330.4 9.9 %all-to-all-start.2 = ((f32[4,8,80]{2,0,1:T(4,128)}), f32[4,8,80]{2,0,1:T(4,128)S(1)}, u32[]{:S(2)}, u32[]{:S(2)}) async-start(f32[4,8,80]{2,0,1:T(4,128)} %copy.105), calls=%async_computation.3 | async-start | bytes 32768 | tf_op jit(solution)/shard_map/all_to_all | solution.py:57
  340.4 73.2 %copy-start.1 = (bf16[128,2048]{1,0:T(8,128)(2,1)S(1)}, bf16[128,2048]{1,0:T(8,128)(2,1)}, u32[]{:S(2)}) copy-start(bf16[128,2048]{1,0:T(8,128)(2,1)} %param.5) | copy-start | bytes 1572868
Sparse Core Ops, SparseCore 0:
  309.4 98.1 reduce-scatter.1
where the time goes:
time: 421 us; the launch traced here: 420 us
  waiting for transfers between devices  294 us (70%)
  matrix products  42.7 us (10%)
  local copies, waits for them, and re-layouts  36.8 us (9%)
  starting transfers between devices  16.8 us (4%)
  other arithmetic  15.9 us (4%)
  between operations  14.2 us (3%)
    all_to_all x1, waiting for transfers between devices, per_device(): lax.all_to_all(outgoing, 'expert', split_axis=1, concat_axis=1, tiled=True)  227 us
    reduce_scatter x1, waiting for transfers between devices, per_device(): lax.psum_scatter(jnp.einsum('esd,esf->def', grad_slots, weighted, preferr...  60.3 us
    dot_general x1, matrix products, per_device(): jnp.einsum('esd,def->esf', grad_slots, down_weight, preferred_element_typ...  20.4 us
    dot_general x1, matrix products, per_device(): jnp.einsum('esd,esf->def', grad_slots, weighted, preferred_element_type=j...  16.8 us
    all_to_all x1, local copies, waits for them, and re-layouts, per_device(): lax.all_to_all(outgoing, 'expert', split_axis=1, concat_axis=1, tiled=True)  10.1 us
    reshape x1, local copies, waits for them, and re-layouts, per_device(): outgoing.reshape(local_experts, expert_count, capacity, outgoing.shape[1])  10 us
    another operation x3, other arithmetic  9.15 us
  transfers between devices with their start and end apart: 4, of which 3 were waited for; matrix products, arithmetic and copies ran while one was open for 12% of the time, Pallas kernels for 0%

commit v1 on v0

v1 whole, which is shorter than its diff:
```python
import functools
import math

import jax
import jax.numpy as jnp
from jax import lax
from jax.experimental import pallas as pl
from jax.experimental.pallas import tpu as pltpu
from jax.sharding import PartitionSpec as P

FIRST_PARTS = (6, 4, 4, 3, 4, 3)
SECOND_PARTS = (6, 2)
BF16 = jnp.bfloat16
F32 = jnp.float32
MIB = 1024 * 1024
LITTLE = pl.CostEstimate(flops=1024, bytes_accessed=1024, transcendentals=0)


def info_of(offset, count):
    place, low, high = 0, 1, count // 2
    while high >= 1:
        place = place + (offset // high) % 2 * low
        low, high = low * 2, high // 2
    return place


def ring_place(index, count):
    return index // 2 if index % 2 == 0 else count - 1 - index // 2


def ring_index(place, count):
    return jnp.where(place < count // 2, 2 * place, 2 * (count - 1 - place) + 1)


def piece_of(source, place, count):
    ahead = (ring_place(source, count) + count - place) % count
    return jnp.where(ahead < count // 2, 2 * ahead, 2 * (count - ahead) - 1)


def source_of(piece, place, count):
    ahead = piece // 2 if piece % 2 == 0 else count - (piece + 1) // 2
    return ring_index((place + ahead) % count, count)


def turn_kernel(units, replicas, own_ref, grad_ref, *refs):
    outs, turned = refs[:-1], refs[-1]
    turned[...] = grad_ref[...].T
    rows = turned.shape[0] // replicas
    for out, parts in zip(outs, units):
        row = 0
        for flip, start, half in parts:
            for part in range(2):
                first = pl.multiple_of((own_ref[1] ^ (flip + part)) * rows + start, 128)
                out[row : row + half, :] = turned[pl.ds(first, half), :]
                row += half


def spread_kernel(
    count, own_ref, info_ref, hidden_ref, spread_ref, place_ref, gate_ref
):
    tokens, cap = spread_ref.shape[1], hidden_ref.shape[1] // count
    top = info_ref.shape[1] // 2
    me = own_ref[0]
    mine = me * pl.num_programs(0) + pl.program_id(0)
    masks, gates = [], []
    for source in range(count):
        info = info_ref[info_of(me ^ source, count)].astype(F32)
        same = info[:top].astype(jnp.int32) == mine
        masks.append(jnp.sum(jnp.where(same, 1.0, 0.0), axis=0, keepdims=True))
        gates.append(jnp.sum(jnp.where(same, info[top:], 0.0), axis=0, keepdims=True))
    mask, gate = jnp.concatenate(masks, axis=0), jnp.concatenate(gates, axis=0)
    before = lax.broadcasted_iota(jnp.int32, (tokens, tokens), 0)
    after = lax.broadcasted_iota(jnp.int32, (tokens, tokens), 1)
    earlier = jnp.where(before < after, 1.0, 0.0).astype(BF16)
    position = jnp.dot(mask.astype(BF16), earlier, preferred_element_type=F32)
    position = jnp.where(mask > 0.0, position, -1.0)
    base = lax.broadcasted_iota(jnp.int32, mask.shape, 0) * cap
    place_ref[0] = jnp.where(mask > 0.0, position.astype(jnp.int32) + base, -1)
    gate_ref[0] = gate
    turned = jnp.concatenate([position, gate], axis=0).T
    slot = lax.broadcasted_iota(jnp.int32, (tokens, cap), 1).astype(F32)
    for source in range(count):
        owns = turned[:, source : source + 1] == slot
        weights = jnp.where(owns, turned[:, count + source : count + source + 1], 0.0).astype(BF16)
        spread_ref[piece_of(source, own_ref[2], count)] = jnp.dot(
            weights, hidden_ref[0, source * cap : (source + 1) * cap, :], preferred_element_type=F32
        ).astype(BF16)


def down_kernel(first, count, *refs):
    piece_refs, spread_ref, outs, grads = refs[:count], refs[count], refs[count + 1 : -1], refs[-1]
    tokens, half = spread_ref.shape[1], grads.shape[0]

    @pl.when(pl.program_id(0) == 0)
    def _():
        for i, piece_ref in enumerate(piece_refs):
            grads[:, i * tokens : (i + 1) * tokens] = piece_ref[first : first + half, :]

    spread = spread_ref[...].reshape(count * tokens, spread_ref.shape[2])
    total = jnp.dot(grads[...], spread, preferred_element_type=F32)
    if outs[0].shape[0] == half and len(outs) > 1:
        total = total + outs[0][...].astype(F32)
        outs = outs[1:]
    row = 0
    for out in outs:
        out[...] = total[row : row + out.shape[0], :].astype(BF16)
        row += out.shape[0]


def up_kernel(units, replicas, count, own_ref, *refs):
    piece_refs, refs = refs[: len(units) * count], refs[len(units) * count :]
    weight_ref, place_ref, gate_ref, hidden_ref, hidden_grad_ref, slot_grad_ref, grads, placed = refs
    local, _, tokens = place_ref.shape
    slots = hidden_ref.shape[1]
    cap = slots // count
    group = 16 // math.gcd(cap, 16)
    rows = grads.shape[1] // replicas
    me, replica = own_ref[0], own_ref[1]
    expert = pl.program_id(0)

    def owned(x, low):
        slot = lax.broadcasted_iota(jnp.int32, (group * cap, tokens), 0) + low * cap
        return [place_ref[x, pl.ds(s, 1), :] == slot for s in range(low, low + group)]

    @pl.when(expert == 0)
    def _():
        for number, parts in enumerate(units):
            for i in range(count):
                turned = piece_refs[number * count + i][...].T
                token = pl.multiple_of(source_of(i, own_ref[2], count) * tokens, tokens)
                row = 0
                for flip, first, half in parts:
                    for part in range(2):
                        column = pl.multiple_of((replica ^ (flip + part)) * rows + first, 128)
                        grads[pl.ds(token, tokens), pl.ds(column, half)] = turned[:, row : row + half]
                        row += half
        for low in range(0, count, group):
            placing = jnp.concatenate(
                [
                    jnp.concatenate([jnp.where(o, 1.0, 0.0).astype(BF16) for o in owned(x, low)], axis=1)
                    for x in range(local)
                ],
                axis=0,
            )
            rows_there = jnp.dot(
                placing, grads[low * tokens : (low + group) * tokens, :], preferred_element_type=F32
            ).astype(BF16)
            for x in range(local):
                placed[x, low * cap : (low + group) * cap, :] = rows_there[
                    x * group * cap : (x + 1) * group * cap, :
                ]

    upstream = jnp.dot(placed[expert], weight_ref[0], preferred_element_type=F32)
    for low in range(0, count, group):
        slice_there = slice(low * cap, (low + group) * cap)
        mine = owned(expert, low)
        weighing = jnp.where(mine[0], gate_ref[expert, low : low + 1, :], 0.0)
        for s in range(1, group):
            weighing = weighing + jnp.where(mine[s], gate_ref[expert, low + s : low + s + 1, :], 0.0)
        gates = jnp.sum(weighing, axis=1, keepdims=True)
        part = upstream[slice_there, :]
        hidden_grad_ref[0, slice_there, :] = (gates * part).astype(BF16)
        slot_grad = jnp.sum(hidden_ref[0, slice_there, :].astype(F32) * part, axis=1, keepdims=True)
        for s in range(group):
            slot_grad_ref[0, pl.ds(me ^ (low + s), 1), :] = jnp.sum(
                jnp.where(mine[s], slot_grad, 0.0), axis=0, keepdims=True
            )


def join_kernel(near_ref, *refs):
    far_refs, out_ref = refs[: len(refs) - 1], refs[-1]
    local, width = out_ref.shape[1:]
    first = 0
    for far_ref in far_refs:
        if len(far_ref.shape) == 3:
            continue
        rows = pl.ds(first, far_ref.shape[0])
        total = near_ref[rows, :].astype(F32) + far_ref[...].astype(F32)
        for x in range(local):
            out_ref[rows, x, :] = total[:, x * width : (x + 1) * width].astype(BF16)
        first += far_ref.shape[0]


def tie(value, *others):
    return lax.optimization_barrier((value,) + others)[0]


SMEM = pl.BlockSpec(memory_space=pltpu.SMEM)


def whole(shape):
    return pl.BlockSpec(shape, lambda *_: (0,) * len(shape), pipeline_mode=pl.Buffered(1))


def vmem(shape):
    return pl.BlockSpec(shape, lambda *_: (0,) * len(shape))


def one_expert(*shape):
    return pl.BlockSpec((1,) + shape, lambda x: (x,) + (0,) * len(shape))


def per_device(grad_out, gates, experts, hidden, down_weight):
    count, replicas = lax.axis_size("expert"), lax.axis_size("replica")
    tokens, width = grad_out.shape
    top = experts.shape[1]
    local, _, slots, hidden_width = hidden.shape
    all_width = local * hidden_width
    rows = width // replicas
    hidden = hidden.reshape(local, slots, hidden_width)
    me = lax.axis_index("expert")
    place = jnp.where(me % 2 == 0, me // 2, count - 1 - me // 2)
    own = jnp.stack([me, lax.axis_index("replica"), place]).astype(jnp.int32)

    share = rows // (sum(FIRST_PARTS) + sum(SECOND_PARTS))
    half, second = share * sum(FIRST_PARTS), share * sum(SECOND_PARTS)
    units = (((2, 0, half),), ((2, half, second), (0, 0, rows)))
    unit_shapes = [
        jax.ShapeDtypeStruct((sum(2 * part[2] for part in parts), tokens), BF16) for parts in units
    ]
    sent = pl.pallas_call(
        functools.partial(turn_kernel, units, replicas),
        out_shape=unit_shapes,
        in_specs=[SMEM, vmem(grad_out.shape)],
        out_specs=[vmem(s.shape) for s in unit_shapes],
        scratch_shapes=[pltpu.VMEM((width, tokens), BF16)],
        compiler_params=pltpu.CompilerParams(vmem_limit_bytes=24 * MIB),
        name="turn_tokens",
    )(own, grad_out)
    info = jnp.concatenate([experts.T.astype(BF16), gates.T], axis=0)

    flips = []
    while 2 ** len(flips) < count:
        flips.insert(0, 2 ** len(flips))

    def hop(held, flip):
        moved = lax.ppermute(held, "expert", [(i, i ^ flip) for i in range(count)])
        return jnp.concatenate([held, moved], axis=0)

    ring = [i for i in range(0, count, 2)] + [i for i in range(count - 1, 0, -2)]
    onward = [(ring[i], ring[(i + 1) % count]) for i in range(count)]
    backward = [(b, a) for a, b in onward]

    def turn_ring(pieces):
        right, left = pieces[-2:] if len(pieces) > 1 else pieces * 2
        moved = [lax.ppermute(right, "expert", onward)]
        if len(pieces) + 1 < count:
            moved.append(lax.ppermute(left, "expert", backward))
        return moved

    def spread_hidden(infos):
        return pl.pallas_call(
            functools.partial(spread_kernel, count),
            grid=(local,),
            out_shape=[
                jax.ShapeDtypeStruct((count, tokens, all_width), BF16),
                jax.ShapeDtypeStruct((local, count, tokens), jnp.int32),
                jax.ShapeDtypeStruct((local, count, tokens), F32),
            ],
            in_specs=[SMEM, whole(infos.shape), one_expert(slots, hidden_width)],
            out_specs=[
                pl.BlockSpec((count, tokens, hidden_width), lambda x: (0, 0, x)),
                one_expert(count, tokens),
                one_expert(count, tokens),
            ],
            compiler_params=pltpu.CompilerParams(vmem_limit_bytes=24 * MIB),
            cost_estimate=LITTLE,
            name="spread_hidden",
        )(own, infos, hidden)

    def down(pieces, spread, first, half, parts=(1,), got=()):
        sizes = [half * part // sum(parts) for part in parts]

        def block(size):
            return pl.BlockSpec((size, hidden_width), lambda x: (0, x))

        return pl.pallas_call(
            functools.partial(down_kernel, first, count),
            grid=(local,),
            out_shape=[jax.ShapeDtypeStruct((size, all_width), BF16) for size in sizes],
            in_specs=[whole(piece.shape) for piece in pieces]
            + [pl.BlockSpec((count, tokens, hidden_width), lambda x: (0, 0, x))]
            + [block(half)] * len(got),
            out_specs=[block(size) for size in sizes],
            scratch_shapes=[pltpu.VMEM((half, count * tokens), BF16)],
            compiler_params=pltpu.CompilerParams(vmem_limit_bytes=24 * MIB),
            cost_estimate=LITTLE,
            name="down_grad",
        )(*pieces, spread, *got)

    def to_mate(give):
        return lax.ppermute(give, "replica", [(i, i ^ 1) for i in range(replicas)])

    def to_far(value):
        return lax.ppermute(value, "replica", [(i, i ^ 2) for i in range(replicas)])

    def up(pieces, weight, place, gate):
        return pl.pallas_call(
            functools.partial(up_kernel, units, replicas, count),
            grid=(local,),
            out_shape=[
                jax.ShapeDtypeStruct(hidden.shape, BF16),
                jax.ShapeDtypeStruct((local, count, tokens), F32),
            ],
            in_specs=[SMEM]
            + [whole(piece.shape) for piece in pieces]
            + [
                one_expert(width, hidden_width),
                whole(place.shape),
                whole(gate.shape),
                one_expert(slots, hidden_width),
            ],
            out_specs=[one_expert(slots, hidden_width), one_expert(count, tokens)],
            scratch_shapes=[
                pltpu.VMEM((count * tokens, width), BF16),
                pltpu.VMEM((local, slots, width), BF16),
            ],
            compiler_params=pltpu.CompilerParams(vmem_limit_bytes=48 * MIB),
            cost_estimate=LITTLE,
            name="hidden_grad",
        )(own, *pieces, weight, place, gate, hidden)

    def join(near, fars, first, *before):
        block = sum(far.shape[0] for far in fars)
        return pl.pallas_call(
            join_kernel,
            grid=(1,),
            out_shape=jax.ShapeDtypeStruct((rows, local, hidden_width), BF16),
            in_specs=[pl.BlockSpec((block, all_width), lambda i: (first // block, 0))]
            + [vmem(far.shape) for far in fars]
            + [pl.BlockSpec(memory_space=pl.ANY)] * len(before),
            out_specs=pl.BlockSpec((block, local, hidden_width), lambda i: (first // block, 0, 0)),
            input_output_aliases={1 + len(fars): 0} if before else {},
            compiler_params=pltpu.CompilerParams(vmem_limit_bytes=32 * MIB),
            cost_estimate=LITTLE,
            name="join",
        )(near, *fars, *before)

    step = lax.optimization_barrier
    infos = tie(info, sent[0])[None]
    first, rest = [sent[0]], [sent[1]]
    for number in range(count // 2):
        moved = turn_ring(first)
        if number < len(flips):
            infos = hop(infos, flips[number])
        if number + 1 < count // 2:
            infos, rest[0], *first = step((infos, rest[0], *first, *moved))
        else:
            first = [*first, *moved]
    for flip in flips[count // 2 :]:
        infos = hop(infos, flip)
    spread, place, gate = spread_hidden(infos)
    spread, *first = step((spread, *first))

    def pass_on(returned, flip):
        stay = returned.reshape(count // (2 * flip), 2, flip, local, tokens)
        moved = lax.ppermute(stay[:, 1], "expert", [(i, i ^ flip) for i in range(count)])
        return jnp.stack([stay[:, 0], moved], axis=1).reshape(count, local, tokens)

    moved = turn_ring(rest)
    (give,) = down(first, spread, half, half)
    give, *rest = step((give, *rest, *moved))
    moved = turn_ring(rest)
    parts = list(down(first, spread, 0, half, FIRST_PARTS, (to_mate(give),)))
    *parts, spread = step((*parts, spread))
    rest = list(step((*rest, *moved)))
    weight = jnp.transpose(tie(down_weight, rest[-1]), (1, 0, 2))
    far_first = [to_far(parts[0])]
    while len(rest) < count:
        moved = turn_ring(rest)
        sent_now = len(far_first) < 3
        if sent_now:
            far_first.append(to_far(parts[len(far_first)]))
            far_first[-2], weight, *rest = step((far_first[-2], weight, *rest, *moved))
        else:
            weight, *rest = step((weight, *rest, *moved))

    far_first.append(to_far(parts[3]))
    (give,) = down(rest, spread, second, second)
    far_first[2], give, spread, *parts = step((far_first[2], give, spread, *parts))
    (own_give,) = down(rest, spread, 2 * second + rows, rows)
    far_first[3], got, own_give, *parts = step((far_first[3], to_mate(give), own_give, *parts))
    far_first.append(to_far(parts[4]))
    sums = down(rest, spread, 0, second, SECOND_PARTS, (got,))
    spread = tie(spread, *sums)
    (near,) = down(rest, spread, 2 * second, rows, (1,), (to_mate(own_give),))
    far_first[4], near, place, *sums = step((far_first[4], near, place, *sums, *parts))[: 3 + len(sums)]
    far_first.append(to_far(parts[5]))
    far_second = [to_far(sums[0])]
    hidden_grad, slot_grad = up(first + rest, weight, place, gate)
    far_first[5], far_second[0], hidden_grad, slot_grad, near = step(
        (far_first[5], far_second[0], hidden_grad, slot_grad, near)
    )
    far_second.append(to_far(sums[1]))

    returned = pass_on(jnp.transpose(slot_grad, (1, 0, 2)), flips[0])
    down_grad = join(near, far_first, 0)
    far_second[1], returned, down_grad = step((far_second[1], returned, down_grad))
    for flip in flips[1:]:
        returned = pass_on(returned, flip)
    down_grad = join(near, far_second, half, down_grad)
    sources = lax.axis_index("expert").astype(jnp.int32) ^ jnp.arange(count, dtype=jnp.int32)
    numbers = (sources[:, None] * local + jnp.arange(local, dtype=jnp.int32)[None]).reshape(-1)
    named = experts.T[:, None, :] == numbers[None, :, None]
    gate_grad = jnp.sum(jnp.where(named, returned.reshape(1, -1, tokens), 0.0), axis=1).T

    return hidden_grad.reshape(local, 1, slots, hidden_width), down_grad, gate_grad


def solution(mesh):
    in_specs = (
        P(("expert", "replica"), None),
        P(("expert", "replica"), None),
        P(("expert", "replica"), None),
        P("expert", "replica", None, None),
        P(None, "expert", None),
    )
    out_specs = (
        P("expert", "replica", None, None),
        P("replica", "expert", None),
        P(("expert", "replica"), None),
    )
    return jax.shard_map(
        per_device, mesh=mesh, in_specs=in_specs, out_specs=out_specs, check_vma=False
    )
```

time: 421 us -> 142 us (0.34)
  waiting for transfers between devices: 294 us -> 42.2 us
  Pallas kernels: 0 us -> 50.8 us
  matrix products: 42.7 us -> 0 us
  local copies, waits for them, and re-layouts: 36.8 us -> 10.8 us
  starting transfers between devices: 16.8 us -> 35.1 us
  other arithmetic: 15.9 us -> 2.24 us
  between operations: 14.2 us -> 0.88 us
    all_to_all x3 -> x0, waiting for transfers between devices: 234 us -> none  [the longest x1 227 us: per_device(): lax.all_to_all(outgoing, 'expert', split_axis=1, concat_axis=1, tiled=True)]
    reduce_scatter x1 -> x0, waiting for transfers between devices: 60.3 us -> none  [per_device(): lax.psum_scatter(jnp.einsum('esd,esf->def', grad_slots, weighted, preferr...]
    pallas_call x0 -> x11, Pallas kernels: none -> 50.8 us  [the longest x6 22.4 us: down(): pl.pallas_call(functools.partial(down_kernel, first, count), grid=(local,...]
    dot_general x3 -> x0, matrix products: 42.7 us -> none  [the longest x1 20.4 us: per_device(): jnp.einsum('esd,def->esf', grad_slots, down_weight, preferred_element_typ...]
    ppermute x0 -> x31, waiting for transfers between devices: none -> 42.2 us  [the longest x8 20.6 us: to_far(): return lax.ppermute(value, 'replica', [(i, i ^ 2) for i in range(replicas)])]
    ppermute x0 -> x31, starting transfers between devices: none -> 35.1 us  [the longest x8 12.7 us: turn_ring(): moved = [lax.ppermute(right, 'expert', onward)]]
    all_to_all x3 -> x0, starting transfers between devices: 16.6 us -> none  [the longest x1 7.25 us: per_device(): lax.all_to_all(out_gates, 'expert', split_axis=1, concat_axis=1, tiled=True)]
    reshape x4 -> x0, local copies, waits for them, and re-layouts: 10.8 us -> none  [the longest x1 10 us: per_device(): outgoing.reshape(local_experts, expert_count, capacity, outgoing.shape[1])]
  transfers between devices with their start and end apart: 4 -> 31, of which waited for: 3 -> 14; matrix products, arithmetic and copies ran while one was open for 12% -> 6% of each run, Pallas kernels for 0% -> 35%
where the time goes in v1:
time: 142 us
  Pallas kernels  50.8 us (36%)
  waiting for transfers between devices  42.2 us (30%)
  starting transfers between devices  35.1 us (25%)
  local copies, waits for them, and re-layouts  10.8 us (8%)
  other arithmetic  2.24 us (2%)
    pallas_call x6, Pallas kernels, down(): pl.pallas_call(functools.partial(down_kernel, first, count), grid=(local,...  22.4 us
    ppermute x8, waiting for transfers between devices, to_far(): return lax.ppermute(value, 'replica', [(i, i ^ 2) for i in range(replicas)])  20.6 us
    pallas_call x1, Pallas kernels, up(): pl.pallas_call(functools.partial(up_kernel, units, replicas, count), grid...  16.7 us
    ppermute x8, starting transfers between devices, turn_ring(): moved = [lax.ppermute(right, 'expert', onward)]  12.7 us
    ppermute x3, waiting for transfers between devices, hop(): moved = lax.ppermute(held, 'expert', [(i, i ^ flip) for i in range(count)])  11.6 us
    ppermute x8, starting transfers between devices, to_far(): return lax.ppermute(value, 'replica', [(i, i ^ 2) for i in range(replicas)])  10.2 us
    optimization_barrier x1, local copies, waits for them, and re-layouts, tie(): return lax.optimization_barrier((value,) + others)[0]  6.45 us
    pallas_call x2, Pallas kernels, join(): pl.pallas_call(join_kernel, grid=(1,), out_shape=jax.ShapeDtypeStruct((ro...  6.08 us
  transfers between devices with their start and end apart: 31, of which 14 were waited for; matrix products, arithmetic and copies ran while one was open for 6% of the time, Pallas kernels for 35%

profile of v1, /device:TPU:0, one launch (start us, length us, event | category | flops | bytes accessed | tf_op | source)
XLA Modules:
  0.0 142.1 jit_solution(14294215496475172146)
XLA Ops:
  0.7 0.1 pad_add_fusion.own_ref
  0.7 1.0 copy-done.3
  1.8 0.8 turn_tokens.1
  2.5 3.1 %collective-permute-start.1 = (bf16[768,128]{1,0:T(8,128)(2,1)S(1)}, bf16[768,128]{1,0:T(8,128)(2,1)S(1)}, u32[]{:S(2)}, u32[]{:S(2)}) collective-permute-start(bf16[768,128]{1,0:T(8,128)(2,1)S(1)} %get-tuple-element.133.refs_0_), channel_id=1, source_target_pairs={{0,8},{8,16},{16,24},{24,28},{28,20},{20,12},{12,4},{4,0},{1,9},{9... | collective-permute-start | bytes 589832 | tf_op jit(solution)/shard_map/ppermute | solution.py:246
  5.6 0.7 bitcast_convert_fusion
  6.3 0.7 pad_maximum_fusion.6
  7.0 3.0 %collective-permute-start = (bf16[1,16,128]{2,1,0:T(8,128)(2,1)S(1)}, bf16[1,16,128]{2,1,0:T(8,128)(2,1)S(1)}, u32[]{:S(2)}, u32[]{:S(2)}) collective-permute-start(bf16[1,16,128]{2,1,0:T(8,128)(2,1)S(1)} %bitcast.46), channel_id=1, source_target_pairs={{0,16},{4,20},{8,24},{12,28},{16,0},{20,4},{24,8},{28,12},{1,17},{... | collective-permute-start | bytes 12296 | tf_op jit(solution)/shard_map/ppermute | solution.py:237
  10.0 3.1 %collective-permute-done = bf16[1,16,128]{2,1,0:T(8,128)(2,1)S(1)} collective-permute-done((bf16[1,16,128]{2,1,0:T(8,128)(2,1)S(1)}, bf16[1,16,128]{2,1,0:T(8,128)(2,1)S(1)}, u32[]{:S(2)}, u32[]{:S(2)}) %collective-permute-start) | collective-permute-done | bytes 4128 | tf_op jit(solution)/shard_map/ppermute | solution.py:237
  13.1 1.6 %collective-permute-start.4 = (bf16[768,128]{1,0:T(8,128)(2,1)S(1)}, bf16[768,128]{1,0:T(8,128)(2,1)S(1)}, u32[]{:S(2)}, u32[]{:S(2)}) collective-permute-start(bf16[768,128]{1,0:T(8,128)(2,1)S(1)} %collective-permute-done.1.refs_1_), channel_id=1, source_target_pairs={{0,8},{8,16},{16,24},{24,28},{28,20},{20,12},{12,4},{4,0},{1,9},{9... | collective-permute-start | bytes 589832 | tf_op jit(solution)/shard_map/ppermute | solution.py:246
  14.7 0.5 collective-permute-start.5
  15.2 1.5 %collective-permute-start.3 = (bf16[2,16,128]{2,1,0:T(8,128)(2,1)S(1)}, bf16[2,16,128]{2,1,0:T(8,128)(2,1)S(1)}, u32[]{:S(2)}, u32[]{:S(2)}) collective-permute-start(bf16[2,16,128]{2,1,0:T(8,128)(2,1)S(1)} %pad_maximum_fusion.5), channel_id=1, source_target_pairs={{0,8},{4,12},{8,0},{12,4},{16,24},{20,28},{24,16},{28,20},{1,9},{5... | collective-permute-start | bytes 24584 | tf_op jit(solution)/shard_map/ppermute | solution.py:237
  16.8 3.7 %collective-permute-done.3 = bf16[2,16,128]{2,1,0:T(8,128)(2,1)S(1)} collective-permute-done((bf16[2,16,128]{2,1,0:T(8,128)(2,1)S(1)}, bf16[2,16,128]{2,1,0:T(8,128)(2,1)S(1)}, u32[]{:S(2)}, u32[]{:S(2)}) %collective-permute-start.3) | collective-permute-done | bytes 8224 | tf_op jit(solution)/shard_map/ppermute | solution.py:237
  20.5 0.4 collective-permute-start.7
  20.8 1.7 %collective-permute-start.8 = (bf16[768,128]{1,0:T(8,128)(2,1)S(1)}, bf16[768,128]{1,0:T(8,128)(2,1)S(1)}, u32[]{:S(2)}, u32[]{:S(2)}) collective-permute-start(bf16[768,128]{1,0:T(8,128)(2,1)S(1)} %collective-permute-done.5.refs_4_), channel_id=1, source_target_pairs={{8,0},{16,8},{24,16},{28,24},{20,28},{12,20},{4,12},{0,4},{9,1},{1... | collective-permute-start | bytes 589832 | tf_op jit(solution)/shard_map/ppermute | solution.py:248
  22.6 0.3 collective-permute-start.6
  22.9 4.7 %collective-permute-done.6 = bf16[4,16,128]{2,1,0:T(8,128)(2,1)S(1)} collective-permute-done((bf16[4,16,128]{2,1,0:T(8,128)(2,1)S(1)}, bf16[4,16,128]{2,1,0:T(8,128)(2,1)S(1)}, u32[]{:S(2)}, u32[]{:S(2)}) %collective-permute-start.6) | collective-permute-done | bytes 16416 | tf_op jit(solution)/shard_map/ppermute | solution.py:237
  27.7 1.2 collective-permute-start.10
  28.8 1.2 collective-permute-start.11
  30.1 1.2 collective-permute-start.9
  31.2 2.1 %copy-done = bf16[4,1,640,768]{3,2,1,0:T(8,128)(2,1)S(1)} copy-done((bf16[4,1,640,768]{3,2,1,0:T(8,128)(2,1)S(1)}, bf16[4,1,640,768]{3,2,1,0:T(8,128)(2,1)}, u32[]{:S(2)}) %copy-start) | copy-done | bytes 3932184
  33.3 4.9 %spread_hidden.1 = (bf16[8,128,3072]{2,1,0:T(8,128)(2,1)S(1)}, s32[4,8,128]{2,1,0:T(8,128)S(1)}, f32[4,8,128]{2,1,0:T(8,128)S(1)}) custom-call(s32[3]{0:T(128)S(1)} %pad_add_fusion.own_ref, bf16[8,16,128]{2,1,0:T(8,128)(2,1)S(1)} %pad_maximum_fusion.info_ref, bf16[4,640,768]{2,1,0:T(8,128)(2,1)S(1)} %bitcast.37), custom_call_target="tpu_custom_call" | custom-call | flops 1024 | bytes 1024 | tf_op jit(solution)/shard_map/spread_hidden/pallas_call | solution.py:252
  38.2 0.0 slice-start.1
  38.2 3.9 %down_grad.6 = bf16[384,3072]{1,0:T(8,128)(2,1)S(1)} custom-call(bf16[768,128]{1,0:T(8,128)(2,1)S(1)} %get-tuple-element.133.refs_0_, bf16[768,128]{1,0:T(8,128)(2,1)S(1)} %collective-permute-done.1.refs_1_, bf16[768,128]{1,0:T(8,128)(2,1)S(1)} %collective-permute-done.2.refs_2_, bf16[768,128]{1,0:T(8,128)(2,1)S(1)} %collective-permute-done.4.refs_3_, ...), custom_call_target="tpu_custom_call" | custom-call | flops 1024 | bytes 1024 | tf_op jit(solution)/shard_map/down_grad/pallas_call | solution.py:277
  42.2 0.1 collective-permute-start.12
  42.3 2.1 %collective-permute-start.17 = (bf16[1280,128]{1,0:T(8,128)(2,1)S(1)}, bf16[1280,128]{1,0:T(8,128)(2,1)S(1)}, u32[]{:S(2)}, u32[]{:S(2)}) collective-permute-start(bf16[1280,128]{1,0:T(8,128)(2,1)S(1)} %collective-permute-done.10.refs_1_.refs_9_), channel_id=1, source_target_pairs={{0,8},{8,16},{16,24},{24,28},{28,20},{20,12},{12,4},{4,0},{1,9},{9... | collective-permute-start | bytes 983048 | tf_op jit(solution)/shard_map/ppermute | solution.py:246
  44.3 0.0 collective-permute-start.18
  44.4 2.4 %collective-permute-done.12.refs_9_ = bf16[384,3072]{1,0:T(8,128)(2,1)S(1)} collective-permute-done((bf16[384,3072]{1,0:T(8,128)(2,1)S(1)}, bf16[384,3072]{1,0:T(8,128)(2,1)S(1)}, u32[]{:S(2)}, u32[]{:S(2)}) %collective-permute-start.12) | collective-permute-done | bytes 2359328 | tf_op jit(solution)/shard_map/ppermute | solution.py:292
  46.8 4.2 %down_grad.7 = (bf16[96,3072]{1,0:T(8,128)(2,1)S(1)}, bf16[64,3072]{1,0:T(8,128)(2,1)S(1)}, bf16[64,3072]{1,0:T(8,128)(2,1)S(1)}, bf16[48,3072]{1,0:T(8,128)(2,1...) custom-call(bf16[768,128]{1,0:T(8,128)(2,1)S(1)} %get-tuple-element.133.refs_0_, ...), custom_call_target="tpu_custom_call" | custom-call | flops 1024 | bytes 1024 | tf_op jit(solution)/shard_map/down_grad/pallas_call | solution.py:277
  51.0 1.6 %collective-permute-start.16 = (bf16[96,3072]{1,0:T(8,128)(2,1)S(1)}, bf16[96,3072]{1,0:T(8,128)(2,1)S(1)}, u32[]{:S(2)}, u32[]{:S(2)}) collective-permute-start(bf16[96,3072]{1,0:T(8,128)(2,1)S(1)} %get-tuple-element.153), channel_id=1, source_target_pairs={{0,2},{1,3},{2,0},{3,1},{4,6},{5,7},{6,4},{7,5},{8,10},{9,11},{10,... | collective-permute-start | bytes 1769480 | tf_op jit(solution)/shard_map/ppermute | solution.py:295
  52.6 1.5 %collective-permute-done.18.refs_4_.refs_12_ = bf16[1280,128]{1,0:T(8,128)(2,1)S(1)} collective-permute-done((bf16[1280,128]{1,0:T(8,128)(2,1)S(1)}, bf16[1280,128]{1,0:T(8,128)(2,1)S(1)}, u32[]{:S(2)}, u32[]{:S(2)}) %collective-permute-start.18) | collective-permute-done | bytes 327712 | tf_op jit(solution)/shard_map/ppermute | solution.py:248
  54.1 1.3 collective-permute-start.19
  55.4 0.8 collective-permute-start.20
  56.2 1.5 %collective-permute-start.15 = (bf16[64,3072]{1,0:T(8,128)(2,1)S(1)}, bf16[64,3072]{1,0:T(8,128)(2,1)S(1)}, u32[]{:S(2)}, u32[]{:S(2)}) collective-permute-start(bf16[64,3072]{1,0:T(8,128)(2,1)S(1)} %get-tuple-element.152), channel_id=1, source_target_pairs={{0,2},{1,3},{2,0},{3,1},{4,6},{5,7},{6,4},{7,5},{8,10},{9,11},{10,... | collective-permute-start | bytes 1179656 | tf_op jit(solution)/shard_map/ppermute | solution.py:295
  57.7 0.5 collective-permute-start.14
  58.2 6.4 %copy.40 = bf16[2048,4,768]{2,0,1:T(8,128)(2,1)} copy(bf16[2048,4,768]{2,1,0:T(4,128)(2,1)S(1)} %bitcast.41) | data formatting | bytes 25165824 | tf_op jit(solution)/shard_map/optimization_barrier | solution.py:185
  64.6 2.6 %collective-permute-done.16.refs_0_ = bf16[96,3072]{1,0:T(8,128)(2,1)S(1)} collective-permute-done((bf16[96,3072]{1,0:T(8,128)(2,1)S(1)}, bf16[96,3072]{1,0:T(8,128)(2,1)S(1)}, u32[]{:S(2)}, u32[]{:S(2)}) %collective-permute-start.16) | collective-permute-done | bytes 589856 | tf_op jit(solution)/shard_map/ppermute | solution.py:295
  67.3 2.0 %collective-permute-start.21 = (bf16[1280,128]{1,0:T(8,128)(2,1)S(1)}, bf16[1280,128]{1,0:T(8,128)(2,1)S(1)}, u32[]{:S(2)}, u32[]{:S(2)}) collective-permute-start(bf16[1280,128]{1,0:T(8,128)(2,1)S(1)} %collective-permute-done.19.refs_5_.refs_13_), channel_id=1, source_target_pairs={{0,8},{8,16},{16,24},{24,28},{28,20},{20,12},{12,4},{4,0},{1,9},{9... | collective-permute-start | bytes 983048 | tf_op jit(solution)/shard_map/ppermute | solution.py:246
  69.3 6.4 %collective-permute-done.15.refs_1_ = bf16[64,3072]{1,0:T(8,128)(2,1)S(1)} collective-permute-done((bf16[64,3072]{1,0:T(8,128)(2,1)S(1)}, bf16[64,3072]{1,0:T(8,128)(2,1)S(1)}, u32[]{:S(2)}, u32[]{:S(2)}) %collective-permute-start.15) | collective-permute-done | bytes 393248 | tf_op jit(solution)/shard_map/ppermute | solution.py:295
  75.7 2.1 %down_grad.8 = bf16[128,3072]{1,0:T(8,128)(2,1)S(1)} custom-call(bf16[1280,128]{1,0:T(8,128)(2,1)S(1)} %get-tuple-element.171.refs_0_.refs_8_, bf16[1280,128]{1,0:T(8,128)(2,1)S(1)} %collective-permute-done.10.refs_1_.refs_9_, bf16[1280,128]{1,0:T(8,128)(2,1)S(1)} %collective-permute-done.11.refs_2_.refs_10_, ...), custom_call_target="tpu_custom_call" | custom-call | flops 1024 | bytes 1024 | tf_op jit(solution)/shard_map/down_grad/pallas_call | solution.py:277
  77.8 5.5 %collective-permute-done.14.refs_2_ = bf16[64,3072]{1,0:T(8,128)(2,1)S(1)} collective-permute-done((bf16[64,3072]{1,0:T(8,128)(2,1)S(1)}, bf16[64,3072]{1,0:T(8,128)(2,1)S(1)}, u32[]{:S(2)}, u32[]{:S(2)}) %collective-permute-start.14) | collective-permute-done | bytes 393248 | tf_op jit(solution)/shard_map/ppermute | solution.py:295
  83.3 1.5 %collective-permute-start.13 = (bf16[48,3072]{1,0:T(8,128)(2,1)S(1)}, bf16[48,3072]{1,0:T(8,128)(2,1)S(1)}, u32[]{:S(2)}, u32[]{:S(2)}) collective-permute-start(bf16[48,3072]{1,0:T(8,128)(2,1)S(1)} %get-tuple-element.150), channel_id=1, source_target_pairs={{0,2},{1,3},{2,0},{3,1},{4,6},{5,7},{6,4},{7,5},{8,10},{9,11},{10,... | collective-permute-start | bytes 884744 | tf_op jit(solution)/shard_map/ppermute | solution.py:295
  84.8 4.8 %down_grad.9 = bf16[512,3072]{1,0:T(8,128)(2,1)S(1)} custom-call(bf16[1280,128]{1,0:T(8,128)(2,1)S(1)} %get-tuple-element.171.refs_0_.refs_8_, bf16[1280,128]{1,0:T(8,128)(2,1)S(1)} %collective-permute-done.10.refs_1_.refs_9_, bf16[1280,128]{1,0:T(8,128)(2,1)S(1)} %collective-permute-done.11.refs_2_.refs_10_, ...), custom_call_target="tpu_custom_call" | custom-call | flops 1024 | bytes 1024 | tf_op jit(solution)/shard_map/down_grad/pallas_call | solution.py:277
  89.7 3.0 %collective-permute-done.13.refs_3_ = bf16[48,3072]{1,0:T(8,128)(2,1)S(1)} collective-permute-done((bf16[48,3072]{1,0:T(8,128)(2,1)S(1)}, bf16[48,3072]{1,0:T(8,128)(2,1)S(1)}, u32[]{:S(2)}, u32[]{:S(2)}) %collective-permute-start.13) | collective-permute-done | bytes 294944 | tf_op jit(solution)/shard_map/ppermute | solution.py:295
  92.7 1.5 %collective-permute-start.24 = (bf16[64,3072]{1,0:T(8,128)(2,1)S(1)}, bf16[64,3072]{1,0:T(8,128)(2,1)S(1)}, u32[]{:S(2)}, u32[]{:S(2)}) collective-permute-start(bf16[64,3072]{1,0:T(8,128)(2,1)S(1)} %get-tuple-element.187), channel_id=1, source_target_pairs={{0,2},{1,3},{2,0},{3,1},{4,6},{5,7},{6,4},{7,5},{8,10},{9,11},{10,... | collective-permute-start | bytes 1179656 | tf_op jit(solution)/shard_map/ppermute | solution.py:295
  94.3 2.2 %down_grad.10 = (bf16[96,3072]{1,0:T(8,128)(2,1)S(1)}, bf16[32,3072]{1,0:T(8,128)(2,1)S(1)}) custom-call(bf16[1280,128]{1,0:T(8,128)(2,1)S(1)} %get-tuple-element.171.refs_0_.refs_8_, bf16[1280,128]{1,0:T(8,128)(2,1)S(1)} %collective-permute-done.10.refs_1_.refs_9_, bf16[1280,128]{1,0:T(8,128)(2,1)S(1)} %collective-permute-done.11.refs_2_.refs_10_, ...), custom_call_target="tpu_custom_call" | custom-call | flops 1024 | bytes 1024 | tf_op jit(solution)/shard_map/down_grad/pallas_call | solution.py:277
  96.4 2.0 %collective-permute-done.25.refs_9_ = bf16[512,3072]{1,0:T(8,128)(2,1)S(1)} collective-permute-done((bf16[512,3072]{1,0:T(8,128)(2,1)S(1)}, bf16[512,3072]{1,0:T(8,128)(2,1)S(1)}, u32[]{:S(2)}, u32[]{:S(2)}) %collective-permute-start.25) | collective-permute-done | bytes 3145760 | tf_op jit(solution)/shard_map/ppermute | solution.py:292
  98.4 5.1 %down_grad.11.near_ref = bf16[512,3072]{1,0:T(8,128)(2,1)S(1)} custom-call(bf16[1280,128]{1,0:T(8,128)(2,1)S(1)} %get-tuple-element.171.refs_0_.refs_8_, bf16[1280,128]{1,0:T(8,128)(2,1)S(1)} %collective-permute-done.10.refs_1_.refs_9_, bf16[1280,128]{1,0:T(8,128)(2,1)S(1)} %collective-permute-done.11.refs_2_.refs_10_, ...), custom_call_target="tpu_custom_call" | custom-call | flops 1024 | bytes 1024 | tf_op jit(solution)/shard_map/down_grad/pallas_call | solution.py:277
  103.5 0.8 collective-permute-done.24.refs_4_
  104.3 1.5 %collective-permute-start.26 = (bf16[96,3072]{1,0:T(8,128)(2,1)S(1)}, bf16[96,3072]{1,0:T(8,128)(2,1)S(1)}, u32[]{:S(2)}, u32[]{:S(2)}) collective-permute-start(bf16[96,3072]{1,0:T(8,128)(2,1)S(1)} %get-tuple-element.194), channel_id=1, source_target_pairs={{0,2},{1,3},{2,0},{3,1},{4,6},{5,7},{6,4},{7,5},{8,10},{9,11},{10,... | collective-permute-start | bytes 1769480 | tf_op jit(solution)/shard_map/ppermute | solution.py:295
  105.8 0.5 collective-permute-start.23
  106.3 1.5 %collective-permute-start.27 = (bf16[32,3072]{1,0:T(8,128)(2,1)S(1)}, bf16[32,3072]{1,0:T(8,128)(2,1)S(1)}, u32[]{:S(2)}, u32[]{:S(2)}) collective-permute-start(bf16[32,3072]{1,0:T(8,128)(2,1)S(1)} %get-tuple-element.204), channel_id=1, source_target_pairs={{0,2},{1,3},{2,0},{3,1},{4,6},{5,7},{6,4},{7,5},{8,10},{9,11},{10,... | collective-permute-start | bytes 589832 | tf_op jit(solution)/shard_map/ppermute | solution.py:295
  107.8 16.7 %hidden_grad.1 = (bf16[4,640,768]{2,1,0:T(8,128)(2,1)}, f32[4,8,128]{2,1,0:T(8,128)S(1)}) custom-call(s32[3]{0:T(128)S(1)} %pad_add_fusion.own_ref, bf16[768,128]{1,0:T(8,128)(2,1)S(1)} %get-tuple-element.133.refs_0_, bf16[768,128]{1,0:T(8,128)(2,1)S(1)} %collective-permute-done.1.refs_1_, bf16[768,128]{1,0:T(8,128)(2,1)S(1)} %collective-permute-done.2.refs_2_, ...), custom_call_target="tpu_custom_call" | custom-call | flops 1024 | bytes 1024 | tf_op jit(solution)/shard_map/hidden_grad/pallas_call | solution.py:298
  124.5 2.3 %collective-permute-done.23.refs_5_ = bf16[48,3072]{1,0:T(8,128)(2,1)S(1)} collective-permute-done((bf16[48,3072]{1,0:T(8,128)(2,1)S(1)}, bf16[48,3072]{1,0:T(8,128)(2,1)S(1)}, u32[]{:S(2)}, u32[]{:S(2)}) %collective-permute-start.23) | collective-permute-done | bytes 294944 | tf_op jit(solution)/shard_map/ppermute | solution.py:295
  126.8 2.8 %collective-permute-start.28 = (f32[1,4,4,128]{3,1,2,0:T(4,128)S(1)}, f32[1,4,4,128]{3,1,2,0:T(4,128)S(1)}, u32[]{:S(2)}, u32[]{:S(2)}) collective-permute-start(f32[1,4,4,128]{3,1,2,0:T(4,128)S(1)} %get-tuple-element.232), channel_id=1, source_target_pairs={{0,16},{4,20},{8,24},{12,28},{16,0},{20,4},{24,8},{28,12},{1,17},{... | collective-permute-start | bytes 24584 | tf_op jit(solution)/shard_map/ppermute | solution.py:357
  129.6 4.2 %join.2.refs_2_ = bf16[512,4,768]{2,1,0:T(4,128)(2,1)} custom-call(bf16[512,3072]{1,0:T(8,128)(2,1)S(1)} %down_grad.11.near_ref, bf16[96,3072]{1,0:T(8,128)(2,1)S(1)} %collective-permute-done.16.refs_0_, bf16[64,3072]{1,0:T(8,128)(2,1)S(1)} %collective-permute-done.15.refs_1_, bf16[64,3072]{1,0:T(8,128)(2,1)S(1)} %collective-permute-done.14.refs_2_, ...), custom_call_target="tpu_custom_call" | custom-call | flops 1024 | bytes 1024 | tf_op jit(solution)/shard_map/join/pallas_call | solution.py:325
  133.9 0.2 collective-permute-start.29
  134.1 3.5 %collective-permute-done.29 = f32[2,2,4,128]{3,2,1,0:T(4,128)S(1)} collective-permute-done((f32[2,2,4,128]{3,2,1,0:T(4,128)S(1)}, f32[2,2,4,128]{3,2,1,0:T(4,128)S(1)}, u32[]{:S(2)}, u32[]{:S(2)}) %collective-permute-start.29) | collective-permute-done | bytes 8224 | tf_op jit(solution)/shard_map/ppermute | solution.py:357
  137.6 0.1 collective-permute-start.30
  137.7 0.1 iota_add_fusion
  137.8 0.1 add.29
  137.9 1.1 copy-done.2
  139.0 1.8 %join.3 = bf16[512,4,768]{2,1,0:T(4,128)(2,1)} custom-call(bf16[512,3072]{1,0:T(8,128)(2,1)S(1)} %down_grad.11.near_ref, bf16[96,3072]{1,0:T(8,128)(2,1)S(1)} %copy-done.2, bf16[32,3072]{1,0:T(8,128)(2,1)S(1)} %collective-permute-done.27.refs_1_, bf16[512,4,768]{2,1,0:T(4,128)(2,1)} %join.2.refs_2_), custom_call_target="tpu_custom_call", output_to_operand_aliasing={{}: (3, {})} | custom-call | flops 1024 | bytes 1024 | tf_op jit(solution)/shard_map/join/pallas_call | solution.py:325
  140.8 0.6 collective-permute-done.30
  141.4 0.7 select_reduce_fusion
  (46 shorter events, 0.1 us)
Async XLA Ops:
  0.7 1.0 copy-start.3
  2.5 10.6 %collective-permute-start.1 = (bf16[768,128]{1,0:T(8,128)(2,1)S(1)}, bf16[768,128]{1,0:T(8,128)(2,1)S(1)}, u32[]{:S(2)}, u32[]{:S(2)}) collective-permute-start(bf16[768,128]{1,0:T(8,128)(2,1)S(1)} %get-tuple-element.133.refs_0_), channel_id=1, source_target_pairs={{0,8},{8,16},{16,24},{24,28},{28,20},{20,12},{12,4},{4,0},{1,9},{9... | collective-permute-start | bytes 589832 | tf_op jit(solution)/shard_map/ppermute | solution.py:246
  5.6 7.5 %collective-permute-start.2 = (bf16[768,128]{1,0:T(8,128)(2,1)S(1)}, bf16[768,128]{1,0:T(8,128)(2,1)S(1)}, u32[]{:S(2)}, u32[]{:S(2)}) collective-permute-start(bf16[768,128]{1,0:T(8,128)(2,1)S(1)} %get-tuple-element.133.refs_0_), channel_id=1, source_target_pairs={{8,0},{16,8},{24,16},{28,24},{20,28},{12,20},{4,12},{0,4},{9,1},{1... | collective-permute-start | bytes 589832 | tf_op jit(solution)/shard_map/ppermute | solution.py:248
  7.0 6.1 %collective-permute-start = (bf16[1,16,128]{2,1,0:T(8,128)(2,1)S(1)}, bf16[1,16,128]{2,1,0:T(8,128)(2,1)S(1)}, u32[]{:S(2)}, u32[]{:S(2)}) collective-permute-start(bf16[1,16,128]{2,1,0:T(8,128)(2,1)S(1)} %bitcast.46), channel_id=1, source_target_pairs={{0,16},{4,20},{8,24},{12,28},{16,0},{20,4},{24,8},{28,12},{1,17},{... | collective-permute-start | bytes 12296 | tf_op jit(solution)/shard_map/ppermute | solution.py:237
  13.1 7.3 %collective-permute-start.4 = (bf16[768,128]{1,0:T(8,128)(2,1)S(1)}, bf16[768,128]{1,0:T(8,128)(2,1)S(1)}, u32[]{:S(2)}, u32[]{:S(2)}) collective-permute-start(bf16[768,128]{1,0:T(8,128)(2,1)S(1)} %collective-permute-done.1.refs_1_), channel_id=1, source_target_pairs={{0,8},{8,16},{16,24},{24,28},{28,20},{20,12},{12,4},{4,0},{1,9},{9... | collective-permute-start | bytes 589832 | tf_op jit(solution)/shard_map/ppermute | solution.py:246
  14.7 5.8 %collective-permute-start.5 = (bf16[768,128]{1,0:T(8,128)(2,1)S(1)}, bf16[768,128]{1,0:T(8,128)(2,1)S(1)}, u32[]{:S(2)}, u32[]{:S(2)}) collective-permute-start(bf16[768,128]{1,0:T(8,128)(2,1)S(1)} %collective-permute-done.2.refs_2_), channel_id=1, source_target_pairs={{8,0},{16,8},{24,16},{28,24},{20,28},{12,20},{4,12},{0,4},{9,1},{1... | collective-permute-start | bytes 589832 | tf_op jit(solution)/shard_map/ppermute | solution.py:248
  15.2 5.3 %collective-permute-start.3 = (bf16[2,16,128]{2,1,0:T(8,128)(2,1)S(1)}, bf16[2,16,128]{2,1,0:T(8,128)(2,1)S(1)}, u32[]{:S(2)}, u32[]{:S(2)}) collective-permute-start(bf16[2,16,128]{2,1,0:T(8,128)(2,1)S(1)} %pad_maximum_fusion.5), channel_id=1, source_target_pairs={{0,8},{4,12},{8,0},{12,4},{16,24},{20,28},{24,16},{28,20},{1,9},{5... | collective-permute-start | bytes 24584 | tf_op jit(solution)/shard_map/ppermute | solution.py:237
  20.5 7.2 %collective-permute-start.7 = (bf16[768,128]{1,0:T(8,128)(2,1)S(1)}, bf16[768,128]{1,0:T(8,128)(2,1)S(1)}, u32[]{:S(2)}, u32[]{:S(2)}) collective-permute-start(bf16[768,128]{1,0:T(8,128)(2,1)S(1)} %collective-permute-done.4.refs_3_), channel_id=1, source_target_pairs={{0,8},{8,16},{16,24},{24,28},{28,20},{20,12},{12,4},{4,0},{1,9},{9... | collective-permute-start | bytes 589832 | tf_op jit(solution)/shard_map/ppermute | solution.py:246
  20.8 6.8 %collective-permute-start.8 = (bf16[768,128]{1,0:T(8,128)(2,1)S(1)}, bf16[768,128]{1,0:T(8,128)(2,1)S(1)}, u32[]{:S(2)}, u32[]{:S(2)}) collective-permute-start(bf16[768,128]{1,0:T(8,128)(2,1)S(1)} %collective-permute-done.5.refs_4_), channel_id=1, source_target_pairs={{8,0},{16,8},{24,16},{28,24},{20,28},{12,20},{4,12},{0,4},{9,1},{1... | collective-permute-start | bytes 589832 | tf_op jit(solution)/shard_map/ppermute | solution.py:248
  22.6 5.1 %collective-permute-start.6 = (bf16[4,16,128]{2,1,0:T(8,128)(2,1)S(1)}, bf16[4,16,128]{2,1,0:T(8,128)(2,1)S(1)}, u32[]{:S(2)}, u32[]{:S(2)}) collective-permute-start(bf16[4,16,128]{2,1,0:T(8,128)(2,1)S(1)} %pad_maximum_fusion.1), channel_id=1, source_target_pairs={{0,4},{4,0},{8,12},{12,8},{16,20},{20,16},{24,28},{28,24},{1,5},{5... | collective-permute-start | bytes 49160 | tf_op jit(solution)/shard_map/ppermute | solution.py:237
  27.7 14.5 %collective-permute-start.10 = (bf16[1280,128]{1,0:T(8,128)(2,1)S(1)}, bf16[1280,128]{1,0:T(8,128)(2,1)S(1)}, u32[]{:S(2)}, u32[]{:S(2)}) collective-permute-start(bf16[1280,128]{1,0:T(8,128)(2,1)S(1)} %get-tuple-element.171.refs_0_.refs_8_), channel_id=1, source_target_pairs={{0,8},{8,16},{16,24},{24,28},{28,20},{20,12},{12,4},{4,0},{1,9},{9... | collective-permute-start | bytes 983048 | tf_op jit(solution)/shard_map/ppermute | solution.py:246
  28.8 13.4 %collective-permute-start.11 = (bf16[1280,128]{1,0:T(8,128)(2,1)S(1)}, bf16[1280,128]{1,0:T(8,128)(2,1)S(1)}, u32[]{:S(2)}, u32[]{:S(2)}) collective-permute-start(bf16[1280,128]{1,0:T(8,128)(2,1)S(1)} %get-tuple-element.171.refs_0_.refs_8_), channel_id=1, source_target_pairs={{8,0},{16,8},{24,16},{28,24},{20,28},{12,20},{4,12},{0,4},{9,1},{1... | collective-permute-start | bytes 983048 | tf_op jit(solution)/shard_map/ppermute | solution.py:248
  30.1 8.1 %collective-permute-start.9 = (bf16[768,128]{1,0:T(8,128)(2,1)S(1)}, bf16[768,128]{1,0:T(8,128)(2,1)S(1)}, u32[]{:S(2)}, u32[]{:S(2)}) collective-permute-start(bf16[768,128]{1,0:T(8,128)(2,1)S(1)} %collective-permute-done.7.refs_5_), channel_id=1, source_target_pairs={{0,8},{8,16},{16,24},{24,28},{28,20},{20,12},{12,4},{4,0},{1,9},{9... | collective-permute-start | bytes 589832 | tf_op jit(solution)/shard_map/ppermute | solution.py:246
  31.2 2.1 %copy-start = (bf16[4,1,640,768]{3,2,1,0:T(8,128)(2,1)S(1)}, bf16[4,1,640,768]{3,2,1,0:T(8,128)(2,1)}, u32[]{:S(2)}) copy-start(bf16[4,1,640,768]{3,2,1,0:T(8,128)(2,1)} %param.8) | copy-start | bytes 11796484
  33.3 24.8 %slice-start = ((s8[12582912]{0:T(1024)(128)(4,1)}), s8[4194304]{0:T(1024)(128)(4,1)S(1)}, s32[]{:S(2)}) async-start(s8[12582912]{0:T(1024)(128)(4,1)} %bitcast.40), calls=%async_computation | async-start | bytes 8388608
  38.2 20.0 %slice-start.1 = ((s8[12582912]{0:T(1024)(128)(4,1)}), s8[4194304]{0:T(1024)(128)(4,1)S(1)}, s32[]{:S(2)}) async-start(s8[12582912]{0:T(1024)(128)(4,1)} %bitcast.40), calls=%async_computation.1 | async-start | bytes 8388608
  42.2 16.0 %slice-start.2 = ((s8[12582912]{0:T(1024)(128)(4,1)}), s8[4194304]{0:T(1024)(128)(4,1)S(1)}, s32[]{:S(2)}) async-start(s8[12582912]{0:T(1024)(128)(4,1)} %bitcast.40), calls=%async_computation.2 | async-start | bytes 8388608
  42.2 4.6 %collective-permute-start.12 = (bf16[384,3072]{1,0:T(8,128)(2,1)S(1)}, bf16[384,3072]{1,0:T(8,128)(2,1)S(1)}, u32[]{:S(2)}, u32[]{:S(2)}) collective-permute-start(bf16[384,3072]{1,0:T(8,128)(2,1)S(1)} %down_grad.6), channel_id=1, source_target_pairs={{0,1},{1,0},{2,3},{3,2},{4,5},{5,4},{6,7},{7,6},{8,9},{9,8},{10,11... | collective-permute-start | bytes 7077896 | tf_op jit(solution)/shard_map/ppermute | solution.py:292
  42.3 10.3 %collective-permute-start.17 = (bf16[1280,128]{1,0:T(8,128)(2,1)S(1)}, bf16[1280,128]{1,0:T(8,128)(2,1)S(1)}, u32[]{:S(2)}, u32[]{:S(2)}) collective-permute-start(bf16[1280,128]{1,0:T(8,128)(2,1)S(1)} %collective-permute-done.10.refs_1_.refs_9_), channel_id=1, source_target_pairs={{0,8},{8,16},{16,24},{24,28},{28,20},{20,12},{12,4},{4,0},{1,9},{9... | collective-permute-start | bytes 983048 | tf_op jit(solution)/shard_map/ppermute | solution.py:246
  44.3 9.8 %collective-permute-start.18 = (bf16[1280,128]{1,0:T(8,128)(2,1)S(1)}, bf16[1280,128]{1,0:T(8,128)(2,1)S(1)}, u32[]{:S(2)}, u32[]{:S(2)}) collective-permute-start(bf16[1280,128]{1,0:T(8,128)(2,1)S(1)} %collective-permute-done.11.refs_2_.refs_10_), channel_id=1, source_target_pairs={{8,0},{16,8},{24,16},{28,24},{20,28},{12,20},{4,12},{0,4},{9,1},{1... | collective-permute-start | bytes 983048 | tf_op jit(solution)/shard_map/ppermute | solution.py:248
  51.0 16.2 %collective-permute-start.16 = (bf16[96,3072]{1,0:T(8,128)(2,1)S(1)}, bf16[96,3072]{1,0:T(8,128)(2,1)S(1)}, u32[]{:S(2)}, u32[]{:S(2)}) collective-permute-start(bf16[96,3072]{1,0:T(8,128)(2,1)S(1)} %get-tuple-element.153), channel_id=1, source_target_pairs={{0,2},{1,3},{2,0},{3,1},{4,6},{5,7},{6,4},{7,5},{8,10},{9,11},{10,... | collective-permute-start | bytes 1769480 | tf_op jit(solution)/shard_map/ppermute | solution.py:295
  54.1 10.5 %collective-permute-start.19 = (bf16[1280,128]{1,0:T(8,128)(2,1)S(1)}, bf16[1280,128]{1,0:T(8,128)(2,1)S(1)}, u32[]{:S(2)}, u32[]{:S(2)}) collective-permute-start(bf16[1280,128]{1,0:T(8,128)(2,1)S(1)} %collective-permute-done.17.refs_3_.refs_11_), channel_id=1, source_target_pairs={{0,8},{8,16},{16,24},{24,28},{28,20},{20,12},{12,4},{4,0},{1,9},{9... | collective-permute-start | bytes 983048 | tf_op jit(solution)/shard_map/ppermute | solution.py:246
  55.4 9.3 %collective-permute-start.20 = (bf16[1280,128]{1,0:T(8,128)(2,1)S(1)}, bf16[1280,128]{1,0:T(8,128)(2,1)S(1)}, u32[]{:S(2)}, u32[]{:S(2)}) collective-permute-start(bf16[1280,128]{1,0:T(8,128)(2,1)S(1)} %collective-permute-done.18.refs_4_.refs_12_), channel_id=1, source_target_pairs={{8,0},{16,8},{24,16},{28,24},{20,28},{12,20},{4,12},{0,4},{9,1},{1... | collective-permute-start | bytes 983048 | tf_op jit(solution)/shard_map/ppermute | solution.py:248
  56.2 19.5 %collective-permute-start.15 = (bf16[64,3072]{1,0:T(8,128)(2,1)S(1)}, bf16[64,3072]{1,0:T(8,128)(2,1)S(1)}, u32[]{:S(2)}, u32[]{:S(2)}) collective-permute-start(bf16[64,3072]{1,0:T(8,128)(2,1)S(1)} %get-tuple-element.152), channel_id=1, source_target_pairs={{0,2},{1,3},{2,0},{3,1},{4,6},{5,7},{6,4},{7,5},{8,10},{9,11},{10,... | collective-permute-start | bytes 1179656 | tf_op jit(solution)/shard_map/ppermute | solution.py:295
  57.7 25.6 %collective-permute-start.14 = (bf16[64,3072]{1,0:T(8,128)(2,1)S(1)}, bf16[64,3072]{1,0:T(8,128)(2,1)S(1)}, u32[]{:S(2)}, u32[]{:S(2)}) collective-permute-start(bf16[64,3072]{1,0:T(8,128)(2,1)S(1)} %get-tuple-element.151), channel_id=1, source_target_pairs={{0,2},{1,3},{2,0},{3,1},{4,6},{5,7},{6,4},{7,5},{8,10},{9,11},{10,... | collective-permute-start | bytes 1179656 | tf_op jit(solution)/shard_map/ppermute | solution.py:295
  67.3 8.4 %collective-permute-start.21 = (bf16[1280,128]{1,0:T(8,128)(2,1)S(1)}, bf16[1280,128]{1,0:T(8,128)(2,1)S(1)}, u32[]{:S(2)}, u32[]{:S(2)}) collective-permute-start(bf16[1280,128]{1,0:T(8,128)(2,1)S(1)} %collective-permute-done.19.refs_5_.refs_13_), channel_id=1, source_target_pairs={{0,8},{8,16},{16,24},{24,28},{28,20},{20,12},{12,4},{4,0},{1,9},{9... | collective-permute-start | bytes 983048 | tf_op jit(solution)/shard_map/ppermute | solution.py:246
  83.3 9.4 %collective-permute-start.22 = (bf16[128,3072]{1,0:T(8,128)(2,1)S(1)}, bf16[128,3072]{1,0:T(8,128)(2,1)S(1)}, u32[]{:S(2)}, u32[]{:S(2)}) collective-permute-start(bf16[128,3072]{1,0:T(8,128)(2,1)S(1)} %down_grad.8), channel_id=1, source_target_pairs={{0,1},{1,0},{2,3},{3,2},{4,5},{5,4},{6,7},{7,6},{8,9},{9,8},{10,11... | collective-permute-start | bytes 2359304 | tf_op jit(solution)/shard_map/ppermute | solution.py:292
  83.3 9.4 %collective-permute-start.13 = (bf16[48,3072]{1,0:T(8,128)(2,1)S(1)}, bf16[48,3072]{1,0:T(8,128)(2,1)S(1)}, u32[]{:S(2)}, u32[]{:S(2)}) collective-permute-start(bf16[48,3072]{1,0:T(8,128)(2,1)S(1)} %get-tuple-element.150), channel_id=1, source_target_pairs={{0,2},{1,3},{2,0},{3,1},{4,6},{5,7},{6,4},{7,5},{8,10},{9,11},{10,... | collective-permute-start | bytes 884744 | tf_op jit(solution)/shard_map/ppermute | solution.py:295
  92.7 5.7 %collective-permute-start.25 = (bf16[512,3072]{1,0:T(8,128)(2,1)S(1)}, bf16[512,3072]{1,0:T(8,128)(2,1)S(1)}, u32[]{:S(2)}, u32[]{:S(2)}) collective-permute-start(bf16[512,3072]{1,0:T(8,128)(2,1)S(1)} %down_grad.9), channel_id=1, source_target_pairs={{0,1},{1,0},{2,3},{3,2},{4,5},{5,4},{6,7},{7,6},{8,9},{9,8},{10,11... | collective-permute-start | bytes 9437192 | tf_op jit(solution)/shard_map/ppermute | solution.py:292
  92.7 11.5 %collective-permute-start.24 = (bf16[64,3072]{1,0:T(8,128)(2,1)S(1)}, bf16[64,3072]{1,0:T(8,128)(2,1)S(1)}, u32[]{:S(2)}, u32[]{:S(2)}) collective-permute-start(bf16[64,3072]{1,0:T(8,128)(2,1)S(1)} %get-tuple-element.187), channel_id=1, source_target_pairs={{0,2},{1,3},{2,0},{3,1},{4,6},{5,7},{6,4},{7,5},{8,10},{9,11},{10,... | collective-permute-start | bytes 1179656 | tf_op jit(solution)/shard_map/ppermute | solution.py:295
  104.3 22.6 %collective-permute-start.26 = (bf16[96,3072]{1,0:T(8,128)(2,1)S(1)}, bf16[96,3072]{1,0:T(8,128)(2,1)S(1)}, u32[]{:S(2)}, u32[]{:S(2)}) collective-permute-start(bf16[96,3072]{1,0:T(8,128)(2,1)S(1)} %get-tuple-element.194), channel_id=1, source_target_pairs={{0,2},{1,3},{2,0},{3,1},{4,6},{5,7},{6,4},{7,5},{8,10},{9,11},{10,... | collective-permute-start | bytes 1769480 | tf_op jit(solution)/shard_map/ppermute | solution.py:295
  105.8 21.0 %collective-permute-start.23 = (bf16[48,3072]{1,0:T(8,128)(2,1)S(1)}, bf16[48,3072]{1,0:T(8,128)(2,1)S(1)}, u32[]{:S(2)}, u32[]{:S(2)}) collective-permute-start(bf16[48,3072]{1,0:T(8,128)(2,1)S(1)} %get-tuple-element.186), channel_id=1, source_target_pairs={{0,2},{1,3},{2,0},{3,1},{4,6},{5,7},{6,4},{7,5},{8,10},{9,11},{10,... | collective-permute-start | bytes 884744 | tf_op jit(solution)/shard_map/ppermute | solution.py:295
  106.3 27.6 %collective-permute-start.27 = (bf16[32,3072]{1,0:T(8,128)(2,1)S(1)}, bf16[32,3072]{1,0:T(8,128)(2,1)S(1)}, u32[]{:S(2)}, u32[]{:S(2)}) collective-permute-start(bf16[32,3072]{1,0:T(8,128)(2,1)S(1)} %get-tuple-element.204), channel_id=1, source_target_pairs={{0,2},{1,3},{2,0},{3,1},{4,6},{5,7},{6,4},{7,5},{8,10},{9,11},{10,... | collective-permute-start | bytes 589832 | tf_op jit(solution)/shard_map/ppermute | solution.py:295
  126.8 7.0 %copy-start.1 = (bf16[96,3072]{1,0:T(8,128)(2,1)}, bf16[96,3072]{1,0:T(8,128)(2,1)S(1)}, u32[]{:S(2)}) copy-start(bf16[96,3072]{1,0:T(8,128)(2,1)S(1)} %collective-permute-done.26.refs_0_) | copy-start | bytes 1769476
  126.8 7.0 %collective-permute-start.28 = (f32[1,4,4,128]{3,1,2,0:T(4,128)S(1)}, f32[1,4,4,128]{3,1,2,0:T(4,128)S(1)}, u32[]{:S(2)}, u32[]{:S(2)}) collective-permute-start(f32[1,4,4,128]{3,1,2,0:T(4,128)S(1)} %get-tuple-element.232), channel_id=1, source_target_pairs={{0,16},{4,20},{8,24},{12,28},{16,0},{20,4},{24,8},{28,12},{1,17},{... | collective-permute-start | bytes 24584 | tf_op jit(solution)/shard_map/ppermute | solution.py:357
  133.9 3.7 %collective-permute-start.29 = (f32[2,2,4,128]{3,2,1,0:T(4,128)S(1)}, f32[2,2,4,128]{3,2,1,0:T(4,128)S(1)}, u32[]{:S(2)}, u32[]{:S(2)}) collective-permute-start(f32[2,2,4,128]{3,2,1,0:T(4,128)S(1)} %bitcast.48), channel_id=1, source_target_pairs={{0,8},{4,12},{8,0},{12,4},{16,24},{20,28},{24,16},{28,20},{1,9},{5... | collective-permute-start | bytes 24584 | tf_op jit(solution)/shard_map/ppermute | solution.py:357
  137.6 3.7 %collective-permute-start.30 = (f32[4,1,4,128]{3,2,0,1:T(4,128)S(1)}, f32[4,1,4,128]{3,2,0,1:T(4,128)S(1)}, u32[]{:S(2)}, u32[]{:S(2)}) collective-permute-start(f32[4,1,4,128]{3,2,0,1:T(4,128)S(1)} %get-tuple-element.228), channel_id=1, source_target_pairs={{0,4},{4,0},{8,12},{12,8},{16,20},{20,16},{24,28},{28,24},{1,5},{5... | collective-permute-start | bytes 24584 | tf_op jit(solution)/shard_map/ppermute | solution.py:357
  137.9 1.1 copy-start.2
  138.9 2.4 %copy-start.4 = (s32[128,8]{0,1:T(8,128)S(1)}, s32[128,8]{0,1:T(8,128)}, u32[]{:S(2)}) copy-start(s32[128,8]{0,1:T(8,128)} %param.7) | copy-start | bytes 12292

commit v2 on v1

--- a/solution.py
+++ b/solution.py
@@ -8,8 +8,8 @@
 from jax.experimental.pallas import tpu as pltpu
 from jax.sharding import PartitionSpec as P
 
-FIRST_PARTS = (6, 4, 4, 3, 4, 3)
-SECOND_PARTS = (6, 2)
+FIRST_PARTS = (6, 4, 3, 3)
+SECOND_PARTS = (8, 4, 4)
 BF16 = jnp.bfloat16
 F32 = jnp.float32
 MIB = 1024 * 1024
@@ -206,6 +206,7 @@
     top = experts.shape[1]
     local, _, slots, hidden_width = hidden.shape
     all_width = local * hidden_width
+    room = min(max(2 * count, 16), 56)
     rows = width // replicas
     hidden = hidden.reshape(local, slots, hidden_width)
     me = lax.axis_index("expert")
@@ -224,7 +225,7 @@
         in_specs=[SMEM, vmem(grad_out.shape)],
         out_specs=[vmem(s.shape) for s in unit_shapes],
         scratch_shapes=[pltpu.VMEM((width, tokens), BF16)],
-        compiler_params=pltpu.CompilerParams(vmem_limit_bytes=24 * MIB),
+        compiler_params=pltpu.CompilerParams(vmem_limit_bytes=56 * MIB),
         name="turn_tokens",
     )(own, grad_out)
     info = jnp.concatenate([experts.T.astype(BF16), gates.T], axis=0)
@@ -263,7 +264,7 @@
                 one_expert(count, tokens),
                 one_expert(count, tokens),
             ],
-            compiler_params=pltpu.CompilerParams(vmem_limit_bytes=24 * MIB),
+            compiler_params=pltpu.CompilerParams(vmem_limit_bytes=room * MIB),
             cost_estimate=LITTLE,
             name="spread_hidden",
         )(own, infos, hidden)
@@ -283,7 +284,7 @@
             + [block(half)] * len(got),
             out_specs=[block(size) for size in sizes],
             scratch_shapes=[pltpu.VMEM((half, count * tokens), BF16)],
-            compiler_params=pltpu.CompilerParams(vmem_limit_bytes=24 * MIB),
+            compiler_params=pltpu.CompilerParams(vmem_limit_bytes=room * MIB),
             cost_estimate=LITTLE,
             name="down_grad",
         )(*pieces, spread, *got)
@@ -315,7 +316,7 @@
                 pltpu.VMEM((count * tokens, width), BF16),
                 pltpu.VMEM((local, slots, width), BF16),
             ],
-            compiler_params=pltpu.CompilerParams(vmem_limit_bytes=48 * MIB),
+            compiler_params=pltpu.CompilerParams(vmem_limit_bytes=min(5 * count, 58) * MIB),
             cost_estimate=LITTLE,
             name="hidden_grad",
         )(own, *pieces, weight, place, gate, hidden)
@@ -331,7 +332,7 @@
             + [pl.BlockSpec(memory_space=pl.ANY)] * len(before),
             out_specs=pl.BlockSpec((block, local, hidden_width), lambda i: (first // block, 0, 0)),
             input_output_aliases={1 + len(fars): 0} if before else {},
-            compiler_params=pltpu.CompilerParams(vmem_limit_bytes=32 * MIB),
+            compiler_params=pltpu.CompilerParams(vmem_limit_bytes=24 * MIB),
             cost_estimate=LITTLE,
             name="join",
         )(near, *fars, *before)
@@ -365,45 +366,39 @@
     *parts, spread = step((*parts, spread))
     rest = list(step((*rest, *moved)))
     weight = jnp.transpose(tie(down_weight, rest[-1]), (1, 0, 2))
-    far_first = [to_far(parts[0])]
+    far_first = [to_far(part) for part in parts[:3]]
+    moved = turn_ring(rest)
+    far_first[0], weight, *rest = step((far_first[0], weight, *rest, *moved))
     while len(rest) < count:
         moved = turn_ring(rest)
-        sent_now = len(far_first) < 3
-        if sent_now:
-            far_first.append(to_far(parts[len(far_first)]))
-            far_first[-2], weight, *rest = step((far_first[-2], weight, *rest, *moved))
-        else:
-            weight, *rest = step((weight, *rest, *moved))
-
-    far_first.append(to_far(parts[3]))
+        far_first[1], *rest = step((far_first[1], *rest, *moved))
+
     (give,) = down(rest, spread, second, second)
     far_first[2], give, spread, *parts = step((far_first[2], give, spread, *parts))
+    far_first.append(to_far(parts[3]))
     (own_give,) = down(rest, spread, 2 * second + rows, rows)
-    far_first[3], got, own_give, *parts = step((far_first[3], to_mate(give), own_give, *parts))
-    far_first.append(to_far(parts[4]))
+    far_first[3], got, own_give, spread = step((far_first[3], to_mate(give), own_give, spread))
     sums = down(rest, spread, 0, second, SECOND_PARTS, (got,))
-    spread = tie(spread, *sums)
-    (near,) = down(rest, spread, 2 * second, rows, (1,), (to_mate(own_give),))
-    far_first[4], near, place, *sums = step((far_first[4], near, place, *sums, *parts))[: 3 + len(sums)]
-    far_first.append(to_far(parts[5]))
-    far_second = [to_far(sums[0])]
+    (near,) = down(rest, tie(spread, *sums), 2 * second, rows, (1,), (to_mate(own_give),))
+    near, place = step((near, place))
+    far_second = [to_far(part) for part in sums]
     hidden_grad, slot_grad = up(first + rest, weight, place, gate)
-    far_first[5], far_second[0], hidden_grad, slot_grad, near = step(
-        (far_first[5], far_second[0], hidden_grad, slot_grad, near)
-    )
-    far_second.append(to_far(sums[1]))
+    far_second[0], hidden_grad, slot_grad, near = step((far_second[0], hidden_grad, slot_grad, near))
 
     returned = pass_on(jnp.transpose(slot_grad, (1, 0, 2)), flips[0])
     down_grad = join(near, far_first, 0)
     far_second[1], returned, down_grad = step((far_second[1], returned, down_grad))
-    for flip in flips[1:]:
+    returned = pass_on(returned, flips[1])
+    down_grad = join(near, far_second[:1], half, down_grad)
+    far_second[2], returned, down_grad = step((far_second[2], returned, down_grad))
+    for flip in flips[2:]:
         returned = pass_on(returned, flip)
-    down_grad = join(near, far_second, half, down_grad)
     sources = lax.axis_index("expert").astype(jnp.int32) ^ jnp.arange(count, dtype=jnp.int32)
     numbers = (sources[:, None] * local + jnp.arange(local, dtype=jnp.int32)[None]).reshape(-1)
     named = experts.T[:, None, :] == numbers[None, :, None]
-    gate_grad = jnp.sum(jnp.where(named, returned.reshape(1, -1, tokens), 0.0), axis=1).T
-
+    gate_grad = jnp.sum(jnp.where(named, returned.reshape(1, -1, tokens), 0.0), axis=1)
+    gate_grad = gate_grad.T
+    down_grad = join(near, far_second[1:], rows - sum(far.shape[0] for far in far_second[1:]), down_grad)
     return hidden_grad.reshape(local, 1, slots, hidden_width), down_grad, gate_grad
 
 

time: 142 us -> 136 us (0.958)
  waiting for transfers between devices: 42.2 us -> 33.4 us
    ppermute x8 -> x7, waiting for transfers between devices: 20.6 us -> 14.4 us  [to_far(): return lax.ppermute(value, 'replica', [(i, i ^ 2) for i in range(replicas)])]
    ppermute x8, waiting for transfers between devices: 0.02 us -> 3.75 us  [turn_ring(): moved = [lax.ppermute(right, 'expert', onward)]]
    ppermute x3, waiting for transfers between devices: 11.6 us -> 8.19 us  [hop(): moved = lax.ppermute(held, 'expert', [(i, i ^ flip) for i in range(count)])]
    ppermute x8, starting transfers between devices: 12.7 us -> 9.88 us  [turn_ring(): moved = [lax.ppermute(right, 'expert', onward)]]
    ppermute x3, waiting for transfers between devices: 4.41 us -> 1.72 us  [to_mate(): return lax.ppermute(give, 'replica', [(i, i ^ 1) for i in range(replicas)])]
    ppermute x3, waiting for transfers between devices: 4.09 us -> 1.59 us  [pass_on(): lax.ppermute(stay[:, 1], 'expert', [(i, i ^ flip) for i in range(count)])]
    ppermute x6, waiting for transfers between devices: 1.53 us -> 3.76 us  [turn_ring(): moved.append(lax.ppermute(left, 'expert', backward))]
    ppermute x6, starting transfers between devices: 4.23 us -> 5.94 us  [turn_ring(): moved.append(lax.ppermute(left, 'expert', backward))]
  transfers between devices with their start and end apart: 31 -> 30, of which waited for: 14 -> 16; matrix products, arithmetic and copies ran while one was open for 6% -> 6% of each run, Pallas kernels for 35% -> 37%
where the time goes in v2:
time: 136 us; the launch traced here: 135 us
  Pallas kernels  52.2 us (38%)
  starting transfers between devices  33.8 us (25%)
  waiting for transfers between devices  33.4 us (25%)
  local copies, waits for them, and re-layouts  11.6 us (9%)
  other arithmetic  3.45 us (3%)
    pallas_call x6, Pallas kernels, down(): pl.pallas_call(functools.partial(down_kernel, first, count), grid=(local,...  22.2 us
    pallas_call x1, Pallas kernels, up(): pl.pallas_call(functools.partial(up_kernel, units, replicas, count), grid...  16.3 us
    ppermute x7, waiting for transfers between devices, to_far(): return lax.ppermute(value, 'replica', [(i, i ^ 2) for i in range(replicas)])  14.4 us
    ppermute x8, starting transfers between devices, turn_ring(): moved = [lax.ppermute(right, 'expert', onward)]  9.88 us
    ppermute x7, starting transfers between devices, to_far(): return lax.ppermute(value, 'replica', [(i, i ^ 2) for i in range(replicas)])  9.75 us
    ppermute x3, waiting for transfers between devices, hop(): moved = lax.ppermute(held, 'expert', [(i, i ^ flip) for i in range(count)])  8.19 us
    pallas_call x3, Pallas kernels, join(): pl.pallas_call(join_kernel, grid=(1,), out_shape=jax.ShapeDtypeStruct((ro...  6.78 us
    optimization_barrier x1, local copies, waits for them, and re-layouts, tie(): return lax.optimization_barrier((value,) + others)[0]  6.42 us
  transfers between devices with their start and end apart: 30, of which 16 were waited for; matrix products, arithmetic and copies ran while one was open for 6% of the time, Pallas kernels for 37%

profile of v2, /device:TPU:0, one launch (start us, length us, event | category | flops | bytes accessed | tf_op | source)
XLA Modules:
  0.0 135.4 jit_solution(1324067174313538589)
XLA Ops:
  0.7 0.6 pad_add_fusion.own_ref
  1.2 2.0 %turn_tokens.1 = (bf16[512,128]{1,0:T(8,128)(2,1)}, bf16[1536,128]{1,0:T(8,128)(2,1)}) custom-call(s32[3]{0:T(128)} %pad_add_fusion.own_ref, bf16[128,2048]{1,0:T(8,128)(2,1)} %grad_ref.1), custom_call_target="tpu_custom_call" | custom-call | tf_op jit(solution)/shard_map/turn_tokens/pallas_call | solution.py:222
  3.3 2.9 %collective-permute-start.2 = (bf16[512,128]{1,0:T(8,128)(2,1)}, bf16[512,128]{1,0:T(8,128)(2,1)S(1)}, u32[]{:S(2)}, u32[]{:S(2)}) collective-permute-start(bf16[512,128]{1,0:T(8,128)(2,1)} %get-tuple-element.126.refs_0_), channel_id=1, source_target_pairs={{8,0},{16,8},{24,16},{28,24},{20,28},{12,20},{4,12},{0,4},{9,1},{1... | collective-permute-start | bytes 393224 | tf_op jit(solution)/shard_map/ppermute | solution.py:249
  6.3 0.7 bitcast_convert_fusion
  7.0 0.7 pad_maximum_fusion.6
  7.7 3.0 %collective-permute-start = (bf16[1,16,128]{2,1,0:T(8,128)(2,1)S(1)}, bf16[1,16,128]{2,1,0:T(8,128)(2,1)S(1)}, u32[]{:S(2)}, u32[]{:S(2)}) collective-permute-start(bf16[1,16,128]{2,1,0:T(8,128)(2,1)S(1)} %bitcast.45), channel_id=1, source_target_pairs={{0,16},{4,20},{8,24},{12,28},{16,0},{20,4},{24,8},{28,12},{1,17},{... | collective-permute-start | bytes 12296 | tf_op jit(solution)/shard_map/ppermute | solution.py:238
  10.7 1.6 %collective-permute-done = bf16[1,16,128]{2,1,0:T(8,128)(2,1)S(1)} collective-permute-done((bf16[1,16,128]{2,1,0:T(8,128)(2,1)S(1)}, bf16[1,16,128]{2,1,0:T(8,128)(2,1)S(1)}, u32[]{:S(2)}, u32[]{:S(2)}) %collective-permute-start) | collective-permute-done | bytes 4128 | tf_op jit(solution)/shard_map/ppermute | solution.py:238
  12.3 2.0 %collective-permute-start.4 = (bf16[512,128]{1,0:T(8,128)(2,1)S(1)}, bf16[512,128]{1,0:T(8,128)(2,1)S(1)}, u32[]{:S(2)}, u32[]{:S(2)}) collective-permute-start(bf16[512,128]{1,0:T(8,128)(2,1)S(1)} %collective-permute-done.1.refs_1_), channel_id=1, source_target_pairs={{0,8},{8,16},{16,24},{24,28},{28,20},{20,12},{12,4},{4,0},{1,9},{9... | collective-permute-start | bytes 393224 | tf_op jit(solution)/shard_map/ppermute | solution.py:247
  14.4 1.9 %collective-permute-start.3 = (bf16[2,16,128]{2,1,0:T(8,128)(2,1)S(1)}, bf16[2,16,128]{2,1,0:T(8,128)(2,1)S(1)}, u32[]{:S(2)}, u32[]{:S(2)}) collective-permute-start(bf16[2,16,128]{2,1,0:T(8,128)(2,1)S(1)} %pad_maximum_fusion.5), channel_id=1, source_target_pairs={{0,8},{4,12},{8,0},{12,4},{16,24},{20,28},{24,16},{28,20},{1,9},{5... | collective-permute-start | bytes 24584 | tf_op jit(solution)/shard_map/ppermute | solution.py:238
  16.3 3.0 %collective-permute-done.3 = bf16[2,16,128]{2,1,0:T(8,128)(2,1)S(1)} collective-permute-done((bf16[2,16,128]{2,1,0:T(8,128)(2,1)S(1)}, bf16[2,16,128]{2,1,0:T(8,128)(2,1)S(1)}, u32[]{:S(2)}, u32[]{:S(2)}) %collective-permute-start.3) | collective-permute-done | bytes 8224 | tf_op jit(solution)/shard_map/ppermute | solution.py:238
  19.4 1.5 %collective-permute-start.7 = (bf16[512,128]{1,0:T(8,128)(2,1)S(1)}, bf16[512,128]{1,0:T(8,128)(2,1)S(1)}, u32[]{:S(2)}, u32[]{:S(2)}) collective-permute-start(bf16[512,128]{1,0:T(8,128)(2,1)S(1)} %collective-permute-done.4.refs_3_), channel_id=1, source_target_pairs={{0,8},{8,16},{16,24},{24,28},{28,20},{20,12},{12,4},{4,0},{1,9},{9... | collective-permute-start | bytes 393224 | tf_op jit(solution)/shard_map/ppermute | solution.py:247
  20.8 0.6 collective-permute-start.8
  21.4 0.6 collective-permute-start.6
  22.0 3.6 %collective-permute-done.6 = bf16[4,16,128]{2,1,0:T(8,128)(2,1)S(1)} collective-permute-done((bf16[4,16,128]{2,1,0:T(8,128)(2,1)S(1)}, bf16[4,16,128]{2,1,0:T(8,128)(2,1)S(1)}, u32[]{:S(2)}, u32[]{:S(2)}) %collective-permute-start.6) | collective-permute-done | bytes 16416 | tf_op jit(solution)/shard_map/ppermute | solution.py:238
  25.6 1.6 %collective-permute-done.8.refs_6_ = bf16[512,128]{1,0:T(8,128)(2,1)S(1)} collective-permute-done((bf16[512,128]{1,0:T(8,128)(2,1)S(1)}, bf16[512,128]{1,0:T(8,128)(2,1)S(1)}, u32[]{:S(2)}, u32[]{:S(2)}) %collective-permute-start.8) | collective-permute-done | bytes 131104 | tf_op jit(solution)/shard_map/ppermute | solution.py:249
  27.1 1.0 collective-permute-start.11
  28.1 1.0 collective-permute-start.10
  29.2 1.7 %collective-permute-start.9 = (bf16[512,128]{1,0:T(8,128)(2,1)S(1)}, bf16[512,128]{1,0:T(8,128)(2,1)S(1)}, u32[]{:S(2)}, u32[]{:S(2)}) collective-permute-start(bf16[512,128]{1,0:T(8,128)(2,1)S(1)} %collective-permute-done.7.refs_5_), channel_id=1, source_target_pairs={{0,8},{8,16},{16,24},{24,28},{28,20},{20,12},{12,4},{4,0},{1,9},{9... | collective-permute-start | bytes 393224 | tf_op jit(solution)/shard_map/ppermute | solution.py:247
  30.9 2.1 %copy-done = bf16[4,1,640,768]{3,2,1,0:T(8,128)(2,1)S(1)} copy-done((bf16[4,1,640,768]{3,2,1,0:T(8,128)(2,1)S(1)}, bf16[4,1,640,768]{3,2,1,0:T(8,128)(2,1)}, u32[]{:S(2)}) %copy-start) | copy-done | bytes 3932184
  33.0 0.6 copy-done.6
  33.6 4.9 %spread_hidden.1 = (bf16[8,128,3072]{2,1,0:T(8,128)(2,1)S(1)}, s32[4,8,128]{2,1,0:T(8,128)S(1)}, f32[4,8,128]{2,1,0:T(8,128)S(1)}) custom-call(s32[3]{0:T(128)S(1)} %copy-done.6, bf16[8,16,128]{2,1,0:T(8,128)(2,1)S(1)} %pad_maximum_fusion.info_ref, bf16[4,640,768]{2,1,0:T(8,128)(2,1)S(1)} %bitcast.37), custom_call_target="tpu_custom_call" | custom-call | flops 1024 | bytes 1024 | tf_op jit(solution)/shard_map/spread_hidden/pallas_call | solution.py:253
  38.5 3.0 %down_grad.6 = bf16[256,3072]{1,0:T(8,128)(2,1)S(1)} custom-call(bf16[512,128]{1,0:T(8,128)(2,1)S(1)} %copy-done.3, bf16[512,128]{1,0:T(8,128)(2,1)S(1)} %collective-permute-done.1.refs_1_, bf16[512,128]{1,0:T(8,128)(2,1)S(1)} %collective-permute-done.2.refs_2_, bf16[512,128]{1,0:T(8,128)(2,1)S(1)} %collective-permute-done.4.refs_3_, ...), custom_call_target="tpu_custom_call" | custom-call | flops 1024 | bytes 1024 | tf_op jit(solution)/shard_map/down_grad/pallas_call | solution.py:278
  41.6 1.8 %collective-permute-start.15 = (bf16[1536,128]{1,0:T(8,128)(2,1)S(1)}, bf16[1536,128]{1,0:T(8,128)(2,1)S(1)}, u32[]{:S(2)}, u32[]{:S(2)}) collective-permute-start(bf16[1536,128]{1,0:T(8,128)(2,1)S(1)} %collective-permute-done.10.refs_1_.refs_9_), channel_id=1, source_target_pairs={{0,8},{8,16},{16,24},{24,28},{28,20},{20,12},{12,4},{4,0},{1,9},{9... | collective-permute-start | bytes 1179656 | tf_op jit(solution)/shard_map/ppermute | solution.py:247
  43.4 0.2 collective-permute-start.16
  43.7 1.3 collective-permute-done.12.refs_9_
  45.0 3.2 %down_grad.7 = (bf16[96,3072]{1,0:T(8,128)(2,1)S(1)}, bf16[64,3072]{1,0:T(8,128)(2,1)S(1)}, bf16[48,3072]{1,0:T(8,128)(2,1)S(1)}, bf16[48,3072]{1,0:T(8,128)(2,1)S(1)}) custom-call(bf16[512,128]{1,0:T(8,128)(2,1)S(1)} %copy-done.3, bf16[512,128]{1,0:T(8,128)(2,1)S(1)} %collective-permute-done.1.refs_1_, bf16[512,128]{1,0:T(8,128)(2,1)S(1)} %collective-permute-done.2.refs_2_, ...), custom_call_target="tpu_custom_call" | custom-call | flops 1024 | bytes 1024 | tf_op jit(solution)/shard_map/down_grad/pallas_call | solution.py:278
  48.2 1.6 %collective-permute-start.14 = (bf16[96,3072]{1,0:T(8,128)(2,1)S(1)}, bf16[96,3072]{1,0:T(8,128)(2,1)S(1)}, u32[]{:S(2)}, u32[]{:S(2)}) collective-permute-start(bf16[96,3072]{1,0:T(8,128)(2,1)S(1)} %get-tuple-element.142), channel_id=1, source_target_pairs={{0,2},{1,3},{2,0},{3,1},{4,6},{5,7},{6,4},{7,5},{8,10},{9,11},{10,... | collective-permute-start | bytes 1769480 | tf_op jit(solution)/shard_map/ppermute | solution.py:296
  49.8 3.3 %collective-permute-done.15.refs_3_.refs_11_ = bf16[1536,128]{1,0:T(8,128)(2,1)S(1)} collective-permute-done((bf16[1536,128]{1,0:T(8,128)(2,1)S(1)}, bf16[1536,128]{1,0:T(8,128)(2,1)S(1)}, u32[]{:S(2)}, u32[]{:S(2)}) %collective-permute-start.15) | collective-permute-done | bytes 393248 | tf_op jit(solution)/shard_map/ppermute | solution.py:247
  53.1 1.5 %collective-permute-done.16.refs_4_.refs_12_ = bf16[1536,128]{1,0:T(8,128)(2,1)S(1)} collective-permute-done((bf16[1536,128]{1,0:T(8,128)(2,1)S(1)}, bf16[1536,128]{1,0:T(8,128)(2,1)S(1)}, u32[]{:S(2)}, u32[]{:S(2)}) %collective-permute-start.16) | collective-permute-done | bytes 393248 | tf_op jit(solution)/shard_map/ppermute | solution.py:249
  54.6 1.0 collective-permute-start.17
  55.6 1.0 collective-permute-start.18
  56.7 6.4 %copy.33 = bf16[2048,4,768]{2,0,1:T(8,128)(2,1)} copy(bf16[2048,4,768]{2,1,0:T(4,128)(2,1)S(1)} %copy-done.7) | data formatting | bytes 25165824 | tf_op jit(solution)/shard_map/optimization_barrier | solution.py:185
  63.1 1.5 %collective-permute-start.13 = (bf16[64,3072]{1,0:T(8,128)(2,1)S(1)}, bf16[64,3072]{1,0:T(8,128)(2,1)S(1)}, u32[]{:S(2)}, u32[]{:S(2)}) collective-permute-start(bf16[64,3072]{1,0:T(8,128)(2,1)S(1)} %get-tuple-element.141), channel_id=1, source_target_pairs={{0,2},{1,3},{2,0},{3,1},{4,6},{5,7},{6,4},{7,5},{8,10},{9,11},{10,... | collective-permute-start | bytes 1179656 | tf_op jit(solution)/shard_map/ppermute | solution.py:296
  64.6 0.4 collective-permute-done.17.refs_5_.refs_13_
  65.0 0.7 collective-permute-done.18.refs_6_.refs_14_
  65.7 0.8 collective-permute-start.19
  66.5 1.5 %collective-permute-start.20 = (bf16[48,3072]{1,0:T(8,128)(2,1)S(1)}, bf16[48,3072]{1,0:T(8,128)(2,1)S(1)}, u32[]{:S(2)}, u32[]{:S(2)}) collective-permute-start(bf16[48,3072]{1,0:T(8,128)(2,1)S(1)} %get-tuple-element.167), channel_id=1, source_target_pairs={{0,2},{1,3},{2,0},{3,1},{4,6},{5,7},{6,4},{7,5},{8,10},{9,11},{10,... | collective-permute-start | bytes 884744 | tf_op jit(solution)/shard_map/ppermute | solution.py:296
  68.0 7.1 %collective-permute-done.13.refs_1_ = bf16[64,3072]{1,0:T(8,128)(2,1)S(1)} collective-permute-done((bf16[64,3072]{1,0:T(8,128)(2,1)S(1)}, bf16[64,3072]{1,0:T(8,128)(2,1)S(1)}, u32[]{:S(2)}, u32[]{:S(2)}) %collective-permute-start.13) | collective-permute-done | bytes 393248 | tf_op jit(solution)/shard_map/ppermute | solution.py:296
  75.1 3.0 %down_grad.8 = bf16[256,3072]{1,0:T(8,128)(2,1)S(1)} custom-call(bf16[1536,128]{1,0:T(8,128)(2,1)S(1)} %copy-done.2, bf16[1536,128]{1,0:T(8,128)(2,1)S(1)} %collective-permute-done.10.refs_1_.refs_9_, bf16[1536,128]{1,0:T(8,128)(2,1)S(1)} %collective-permute-done.11.refs_2_.refs_10_, bf16[1536,128]{1,0:T(8,128)(2,1)S(1)} %collective-permute-done.15.refs_3_.refs_11_, ...), custom_call_target="tpu_custom_call" | custom-call | flops 1024 | bytes 1024 | tf_op jit(solution)/shard_map/down_grad/pallas_call | solution.py:278
  78.1 1.1 collective-permute-done.20.refs_2_
  79.2 1.5 %collective-permute-start.21 = (bf16[48,3072]{1,0:T(8,128)(2,1)S(1)}, bf16[48,3072]{1,0:T(8,128)(2,1)S(1)}, u32[]{:S(2)}, u32[]{:S(2)}) collective-permute-start(bf16[48,3072]{1,0:T(8,128)(2,1)S(1)} %get-tuple-element.170), channel_id=1, source_target_pairs={{0,2},{1,3},{2,0},{3,1},{4,6},{5,7},{6,4},{7,5},{8,10},{9,11},{10,... | collective-permute-start | bytes 884744 | tf_op jit(solution)/shard_map/ppermute | solution.py:296
  80.7 4.8 %down_grad.9 = bf16[512,3072]{1,0:T(8,128)(2,1)S(1)} custom-call(bf16[1536,128]{1,0:T(8,128)(2,1)S(1)} %copy-done.2, bf16[1536,128]{1,0:T(8,128)(2,1)S(1)} %collective-permute-done.10.refs_1_.refs_9_, bf16[1536,128]{1,0:T(8,128)(2,1)S(1)} %collective-permute-done.11.refs_2_.refs_10_, bf16[1536,128]{1,0:T(8,128)(2,1)S(1)} %collective-permute-done.15.refs_3_.refs_11_, ...), custom_call_target="tpu_custom_call" | custom-call | flops 1024 | bytes 1024 | tf_op jit(solution)/shard_map/down_grad/pallas_call | solution.py:278
  85.6 3.1 %collective-permute-done.21.refs_3_ = bf16[48,3072]{1,0:T(8,128)(2,1)S(1)} collective-permute-done((bf16[48,3072]{1,0:T(8,128)(2,1)S(1)}, bf16[48,3072]{1,0:T(8,128)(2,1)S(1)}, u32[]{:S(2)}, u32[]{:S(2)}) %collective-permute-start.21) | collective-permute-done | bytes 294944 | tf_op jit(solution)/shard_map/ppermute | solution.py:296
  88.6 3.2 %down_grad.10 = (bf16[128,3072]{1,0:T(8,128)(2,1)S(1)}, bf16[64,3072]{1,0:T(8,128)(2,1)S(1)}, bf16[64,3072]{1,0:T(8,128)(2,1)S(1)}) custom-call(bf16[1536,128]{1,0:T(8,128)(2,1)S(1)} %copy-done.2, bf16[1536,128]{1,0:T(8,128)(2,1)S(1)} %collective-permute-done.10.refs_1_.refs_9_, bf16[1536,128]{1,0:T(8,128)(2,1)S(1)} %collective-permute-done.11.refs_2_.refs_10_, ...), custom_call_target="tpu_custom_call" | custom-call | flops 1024 | bytes 1024 | tf_op jit(solution)/shard_map/down_grad/pallas_call | solution.py:278
  91.8 1.6 %collective-permute-start.23 = (bf16[128,3072]{1,0:T(8,128)(2,1)S(1)}, bf16[128,3072]{1,0:T(8,128)(2,1)S(1)}, u32[]{:S(2)}, u32[]{:S(2)}) collective-permute-start(bf16[128,3072]{1,0:T(8,128)(2,1)S(1)} %get-tuple-element.175), channel_id=1, source_target_pairs={{0,2},{1,3},{2,0},{3,1},{4,6},{5,7},{6,4},{7,5},{8,10},{9,11},{10,... | collective-permute-start | bytes 2359304 | tf_op jit(solution)/shard_map/ppermute | solution.py:296
  93.4 0.5 collective-permute-start.25
  93.9 0.4 collective-permute-done.24.refs_9_
  94.3 5.1 %down_grad.11.near_ref = bf16[512,3072]{1,0:T(8,128)(2,1)S(1)} custom-call(bf16[1536,128]{1,0:T(8,128)(2,1)S(1)} %copy-done.2, bf16[1536,128]{1,0:T(8,128)(2,1)S(1)} %collective-permute-done.10.refs_1_.refs_9_, bf16[1536,128]{1,0:T(8,128)(2,1)S(1)} %collective-permute-done.11.refs_2_.refs_10_, ...), custom_call_target="tpu_custom_call" | custom-call | flops 1024 | bytes 1024 | tf_op jit(solution)/shard_map/down_grad/pallas_call | solution.py:278
  99.4 16.3 %hidden_grad.1 = (bf16[4,640,768]{2,1,0:T(8,128)(2,1)}, f32[4,8,128]{2,1,0:T(8,128)S(1)}) custom-call(s32[3]{0:T(128)S(1)} %copy-done.6, bf16[512,128]{1,0:T(8,128)(2,1)S(1)} %copy-done.3, bf16[512,128]{1,0:T(8,128)(2,1)S(1)} %collective-permute-done.1.refs_1_, bf16[512,128]{1,0:T(8,128)(2,1)S(1)} %collective-permute-done.2.refs_2_, ...), custom_call_target="tpu_custom_call" | custom-call | flops 1024 | bytes 1024 | tf_op jit(solution)/shard_map/hidden_grad/pallas_call | solution.py:299
  115.7 1.5 %collective-permute-start.26 = (f32[1,4,4,128]{3,1,2,0:T(4,128)S(1)}, f32[1,4,4,128]{3,1,2,0:T(4,128)S(1)}, u32[]{:S(2)}, u32[]{:S(2)}) collective-permute-start(f32[1,4,4,128]{3,1,2,0:T(4,128)S(1)} %get-tuple-element.215), channel_id=1, source_target_pairs={{0,16},{4,20},{8,24},{12,28},{16,0},{20,4},{24,8},{28,12},{1,17},{... | collective-permute-start | bytes 24584 | tf_op jit(solution)/shard_map/ppermute | solution.py:358
  117.2 1.5 %collective-permute-start.27 = (bf16[64,3072]{1,0:T(8,128)(2,1)S(1)}, bf16[64,3072]{1,0:T(8,128)(2,1)S(1)}, u32[]{:S(2)}, u32[]{:S(2)}) collective-permute-start(bf16[64,3072]{1,0:T(8,128)(2,1)S(1)} %get-tuple-element.178), channel_id=1, source_target_pairs={{0,2},{1,3},{2,0},{3,1},{4,6},{5,7},{6,4},{7,5},{8,10},{9,11},{10,... | collective-permute-start | bytes 1179656 | tf_op jit(solution)/shard_map/ppermute | solution.py:296
  118.7 3.0 %join.3.refs_1_ = bf16[512,4,768]{2,1,0:T(4,128)(2,1)} custom-call(bf16[512,3072]{1,0:T(8,128)(2,1)S(1)} %down_grad.11.near_ref, bf16[96,3072]{1,0:T(8,128)(2,1)S(1)} %collective-permute-done.14.refs_0_, bf16[64,3072]{1,0:T(8,128)(2,1)S(1)} %collective-permute-done.13.refs_1_, bf16[48,3072]{1,0:T(8,128)(2,1)S(1)} %collective-permute-done.20.refs_2_, ...), custom_call_target="tpu_custom_call" | custom-call | flops 1024 | bytes 1024 | tf_op jit(solution)/shard_map/join/pallas_call | solution.py:326
  121.8 0.9 collective-permute-start.28
  122.6 1.9 %join.4.refs_2_ = bf16[512,4,768]{2,1,0:T(4,128)(2,1)} custom-call(bf16[512,3072]{1,0:T(8,128)(2,1)S(1)} %down_grad.11.near_ref, bf16[128,3072]{1,0:T(8,128)(2,1)S(1)} %collective-permute-done.23.refs_0_, bf16[512,4,768]{2,1,0:T(4,128)(2,1)} %join.3.refs_1_), custom_call_target="tpu_custom_call", output_to_operand_aliasing={{}: (2, {})} | custom-call | flops 1024 | bytes 1024 | tf_op jit(solution)/shard_map/join/pallas_call | solution.py:326
  124.5 0.9 collective-permute-done.28
  125.5 3.2 %collective-permute-done.27.refs_1_ = bf16[64,3072]{1,0:T(8,128)(2,1)S(1)} collective-permute-done((bf16[64,3072]{1,0:T(8,128)(2,1)S(1)}, bf16[64,3072]{1,0:T(8,128)(2,1)S(1)}, u32[]{:S(2)}, u32[]{:S(2)}) %collective-permute-start.27) | collective-permute-done | bytes 393248 | tf_op jit(solution)/shard_map/ppermute | solution.py:296
  128.7 0.7 copy-done.4
  129.4 0.6 copy.34
  130.0 0.3 collective-permute-start.29
  130.5 1.0 copy-done.5
  131.5 1.8 %join.5 = bf16[512,4,768]{2,1,0:T(4,128)(2,1)} custom-call(bf16[512,3072]{1,0:T(8,128)(2,1)S(1)} %down_grad.11.near_ref, bf16[64,3072]{1,0:T(8,128)(2,1)S(1)} %collective-permute-done.25.refs_0_, bf16[64,3072]{1,0:T(8,128)(2,1)S(1)} %copy-done.5, bf16[512,4,768]{2,1,0:T(4,128)(2,1)} %join.4.refs_2_), custom_call_target="tpu_custom_call", output_to_operand_aliasing={{}: (3, {})} | custom-call | flops 1024 | bytes 1024 | tf_op jit(solution)/shard_map/join/pallas_call | solution.py:326
  133.3 0.7 collective-permute-done.29
  134.0 0.7 pad_maximum_fusion.4
  134.7 0.7 select_reduce_fusion
  (45 shorter events, 0.6 us)
Async XLA Ops:
  3.3 35.2 %copy-start.3 = (bf16[512,128]{1,0:T(8,128)(2,1)S(1)}, bf16[512,128]{1,0:T(8,128)(2,1)}, u32[]{:S(2)}) copy-start(bf16[512,128]{1,0:T(8,128)(2,1)} %get-tuple-element.126.refs_0_) | copy-start | bytes 393220
  3.3 9.0 %collective-permute-start.2 = (bf16[512,128]{1,0:T(8,128)(2,1)}, bf16[512,128]{1,0:T(8,128)(2,1)S(1)}, u32[]{:S(2)}, u32[]{:S(2)}) collective-permute-start(bf16[512,128]{1,0:T(8,128)(2,1)} %get-tuple-element.126.refs_0_), channel_id=1, source_target_pairs={{8,0},{16,8},{24,16},{28,24},{20,28},{12,20},{4,12},{0,4},{9,1},{1... | collective-permute-start | bytes 393224 | tf_op jit(solution)/shard_map/ppermute | solution.py:249
  6.2 6.1 %collective-permute-start.1 = (bf16[512,128]{1,0:T(8,128)(2,1)}, bf16[512,128]{1,0:T(8,128)(2,1)S(1)}, u32[]{:S(2)}, u32[]{:S(2)}) collective-permute-start(bf16[512,128]{1,0:T(8,128)(2,1)} %get-tuple-element.126.refs_0_), channel_id=1, source_target_pairs={{0,8},{8,16},{16,24},{24,28},{28,20},{20,12},{12,4},{4,0},{1,9},{9... | collective-permute-start | bytes 393224 | tf_op jit(solution)/shard_map/ppermute | solution.py:247
  7.7 4.6 %collective-permute-start = (bf16[1,16,128]{2,1,0:T(8,128)(2,1)S(1)}, bf16[1,16,128]{2,1,0:T(8,128)(2,1)S(1)}, u32[]{:S(2)}, u32[]{:S(2)}) collective-permute-start(bf16[1,16,128]{2,1,0:T(8,128)(2,1)S(1)} %bitcast.45), channel_id=1, source_target_pairs={{0,16},{4,20},{8,24},{12,28},{16,0},{20,4},{24,8},{28,12},{1,17},{... | collective-permute-start | bytes 12296 | tf_op jit(solution)/shard_map/ppermute | solution.py:238
  12.3 7.0 %collective-permute-start.4 = (bf16[512,128]{1,0:T(8,128)(2,1)S(1)}, bf16[512,128]{1,0:T(8,128)(2,1)S(1)}, u32[]{:S(2)}, u32[]{:S(2)}) collective-permute-start(bf16[512,128]{1,0:T(8,128)(2,1)S(1)} %collective-permute-done.1.refs_1_), channel_id=1, source_target_pairs={{0,8},{8,16},{16,24},{24,28},{28,20},{20,12},{12,4},{4,0},{1,9},{9... | collective-permute-start | bytes 393224 | tf_op jit(solution)/shard_map/ppermute | solution.py:247
  14.3 5.1 %collective-permute-start.5 = (bf16[512,128]{1,0:T(8,128)(2,1)S(1)}, bf16[512,128]{1,0:T(8,128)(2,1)S(1)}, u32[]{:S(2)}, u32[]{:S(2)}) collective-permute-start(bf16[512,128]{1,0:T(8,128)(2,1)S(1)} %collective-permute-done.2.refs_2_), channel_id=1, source_target_pairs={{8,0},{16,8},{24,16},{28,24},{20,28},{12,20},{4,12},{0,4},{9,1},{1... | collective-permute-start | bytes 393224 | tf_op jit(solution)/shard_map/ppermute | solution.py:249
  14.4 4.9 %collective-permute-start.3 = (bf16[2,16,128]{2,1,0:T(8,128)(2,1)S(1)}, bf16[2,16,128]{2,1,0:T(8,128)(2,1)S(1)}, u32[]{:S(2)}, u32[]{:S(2)}) collective-permute-start(bf16[2,16,128]{2,1,0:T(8,128)(2,1)S(1)} %pad_maximum_fusion.5), channel_id=1, source_target_pairs={{0,8},{4,12},{8,0},{12,4},{16,24},{20,28},{24,16},{28,20},{1,9},{5... | collective-permute-start | bytes 24584 | tf_op jit(solution)/shard_map/ppermute | solution.py:238
  19.4 6.2 %collective-permute-start.7 = (bf16[512,128]{1,0:T(8,128)(2,1)S(1)}, bf16[512,128]{1,0:T(8,128)(2,1)S(1)}, u32[]{:S(2)}, u32[]{:S(2)}) collective-permute-start(bf16[512,128]{1,0:T(8,128)(2,1)S(1)} %collective-permute-done.4.refs_3_), channel_id=1, source_target_pairs={{0,8},{8,16},{16,24},{24,28},{28,20},{20,12},{12,4},{4,0},{1,9},{9... | collective-permute-start | bytes 393224 | tf_op jit(solution)/shard_map/ppermute | solution.py:247
  20.8 6.3 %collective-permute-start.8 = (bf16[512,128]{1,0:T(8,128)(2,1)S(1)}, bf16[512,128]{1,0:T(8,128)(2,1)S(1)}, u32[]{:S(2)}, u32[]{:S(2)}) collective-permute-start(bf16[512,128]{1,0:T(8,128)(2,1)S(1)} %collective-permute-done.5.refs_4_), channel_id=1, source_target_pairs={{8,0},{16,8},{24,16},{28,24},{20,28},{12,20},{4,12},{0,4},{9,1},{1... | collective-permute-start | bytes 393224 | tf_op jit(solution)/shard_map/ppermute | solution.py:249
  21.4 4.1 %collective-permute-start.6 = (bf16[4,16,128]{2,1,0:T(8,128)(2,1)S(1)}, bf16[4,16,128]{2,1,0:T(8,128)(2,1)S(1)}, u32[]{:S(2)}, u32[]{:S(2)}) collective-permute-start(bf16[4,16,128]{2,1,0:T(8,128)(2,1)S(1)} %pad_maximum_fusion.1), channel_id=1, source_target_pairs={{0,4},{4,0},{8,12},{12,8},{16,20},{20,16},{24,28},{28,24},{1,5},{5... | collective-permute-start | bytes 49160 | tf_op jit(solution)/shard_map/ppermute | solution.py:238
  27.1 14.4 %collective-permute-start.11 = (bf16[1536,128]{1,0:T(8,128)(2,1)}, bf16[1536,128]{1,0:T(8,128)(2,1)S(1)}, u32[]{:S(2)}, u32[]{:S(2)}) collective-permute-start(bf16[1536,128]{1,0:T(8,128)(2,1)} %get-tuple-element.159.refs_0_.refs_8_), channel_id=1, source_target_pairs={{8,0},{16,8},{24,16},{28,24},{20,28},{12,20},{4,12},{0,4},{9,1},{1... | collective-permute-start | bytes 1179656 | tf_op jit(solution)/shard_map/ppermute | solution.py:249
  28.1 13.4 %collective-permute-start.10 = (bf16[1536,128]{1,0:T(8,128)(2,1)}, bf16[1536,128]{1,0:T(8,128)(2,1)S(1)}, u32[]{:S(2)}, u32[]{:S(2)}) collective-permute-start(bf16[1536,128]{1,0:T(8,128)(2,1)} %get-tuple-element.159.refs_0_.refs_8_), channel_id=1, source_target_pairs={{0,8},{8,16},{16,24},{24,28},{28,20},{20,12},{12,4},{4,0},{1,9},{9... | collective-permute-start | bytes 1179656 | tf_op jit(solution)/shard_map/ppermute | solution.py:247
  29.2 9.3 %collective-permute-start.9 = (bf16[512,128]{1,0:T(8,128)(2,1)S(1)}, bf16[512,128]{1,0:T(8,128)(2,1)S(1)}, u32[]{:S(2)}, u32[]{:S(2)}) collective-permute-start(bf16[512,128]{1,0:T(8,128)(2,1)S(1)} %collective-permute-done.7.refs_5_), channel_id=1, source_target_pairs={{0,8},{8,16},{16,24},{24,28},{28,20},{20,12},{12,4},{4,0},{1,9},{9... | collective-permute-start | bytes 393224 | tf_op jit(solution)/shard_map/ppermute | solution.py:247
  30.9 2.1 %copy-start = (bf16[4,1,640,768]{3,2,1,0:T(8,128)(2,1)S(1)}, bf16[4,1,640,768]{3,2,1,0:T(8,128)(2,1)}, u32[]{:S(2)}) copy-start(bf16[4,1,640,768]{3,2,1,0:T(8,128)(2,1)} %param.8) | copy-start | bytes 11796484
  33.0 0.6 copy-start.6
  38.5 18.2 %copy-start.7 = (bf16[2048,4,768]{2,1,0:T(4,128)(2,1)S(1)}, bf16[2048,4,768]{2,1,0:T(4,128)(2,1)}, u32[]{:S(2)}) copy-start(bf16[2048,4,768]{2,1,0:T(4,128)(2,1)} %param.9) | copy-start | bytes 37748740
  41.5 3.5 %collective-permute-start.12 = (bf16[256,3072]{1,0:T(8,128)(2,1)S(1)}, bf16[256,3072]{1,0:T(8,128)(2,1)S(1)}, u32[]{:S(2)}, u32[]{:S(2)}) collective-permute-start(bf16[256,3072]{1,0:T(8,128)(2,1)S(1)} %down_grad.6), channel_id=1, source_target_pairs={{0,1},{1,0},{2,3},{3,2},{4,5},{5,4},{6,7},{7,6},{8,9},{9,8},{10,11... | collective-permute-start | bytes 4718600 | tf_op jit(solution)/shard_map/ppermute | solution.py:293
  41.6 11.5 %collective-permute-start.15 = (bf16[1536,128]{1,0:T(8,128)(2,1)S(1)}, bf16[1536,128]{1,0:T(8,128)(2,1)S(1)}, u32[]{:S(2)}, u32[]{:S(2)}) collective-permute-start(bf16[1536,128]{1,0:T(8,128)(2,1)S(1)} %collective-permute-done.10.refs_1_.refs_9_), channel_id=1, source_target_pairs={{0,8},{8,16},{16,24},{24,28},{28,20},{20,12},{12,4},{4,0},{1,9},{9... | collective-permute-start | bytes 1179656 | tf_op jit(solution)/shard_map/ppermute | solution.py:247
  43.4 11.2 %collective-permute-start.16 = (bf16[1536,128]{1,0:T(8,128)(2,1)S(1)}, bf16[1536,128]{1,0:T(8,128)(2,1)S(1)}, u32[]{:S(2)}, u32[]{:S(2)}) collective-permute-start(bf16[1536,128]{1,0:T(8,128)(2,1)S(1)} %collective-permute-done.11.refs_2_.refs_10_), channel_id=1, source_target_pairs={{8,0},{16,8},{24,16},{28,24},{20,28},{12,20},{4,12},{0,4},{9,1},{1... | collective-permute-start | bytes 1179656 | tf_op jit(solution)/shard_map/ppermute | solution.py:249
  48.2 26.9 %copy-start.2 = (bf16[1536,128]{1,0:T(8,128)(2,1)S(1)}, bf16[1536,128]{1,0:T(8,128)(2,1)}, u32[]{:S(2)}) copy-start(bf16[1536,128]{1,0:T(8,128)(2,1)} %get-tuple-element.159.refs_0_.refs_8_) | copy-start | bytes 1179652
  48.2 17.5 %collective-permute-start.14 = (bf16[96,3072]{1,0:T(8,128)(2,1)S(1)}, bf16[96,3072]{1,0:T(8,128)(2,1)S(1)}, u32[]{:S(2)}, u32[]{:S(2)}) collective-permute-start(bf16[96,3072]{1,0:T(8,128)(2,1)S(1)} %get-tuple-element.142), channel_id=1, source_target_pairs={{0,2},{1,3},{2,0},{3,1},{4,6},{5,7},{6,4},{7,5},{8,10},{9,11},{10,... | collective-permute-start | bytes 1769480 | tf_op jit(solution)/shard_map/ppermute | solution.py:296
  54.6 10.4 %collective-permute-start.17 = (bf16[1536,128]{1,0:T(8,128)(2,1)S(1)}, bf16[1536,128]{1,0:T(8,128)(2,1)S(1)}, u32[]{:S(2)}, u32[]{:S(2)}) collective-permute-start(bf16[1536,128]{1,0:T(8,128)(2,1)S(1)} %collective-permute-done.15.refs_3_.refs_11_), channel_id=1, source_target_pairs={{0,8},{8,16},{16,24},{24,28},{28,20},{20,12},{12,4},{4,0},{1,9},{9... | collective-permute-start | bytes 1179656 | tf_op jit(solution)/shard_map/ppermute | solution.py:247
  55.6 10.1 %collective-permute-start.18 = (bf16[1536,128]{1,0:T(8,128)(2,1)S(1)}, bf16[1536,128]{1,0:T(8,128)(2,1)S(1)}, u32[]{:S(2)}, u32[]{:S(2)}) collective-permute-start(bf16[1536,128]{1,0:T(8,128)(2,1)S(1)} %collective-permute-done.16.refs_4_.refs_12_), channel_id=1, source_target_pairs={{8,0},{16,8},{24,16},{28,24},{20,28},{12,20},{4,12},{0,4},{9,1},{1... | collective-permute-start | bytes 1179656 | tf_op jit(solution)/shard_map/ppermute | solution.py:249
  63.1 12.1 %collective-permute-start.13 = (bf16[64,3072]{1,0:T(8,128)(2,1)S(1)}, bf16[64,3072]{1,0:T(8,128)(2,1)S(1)}, u32[]{:S(2)}, u32[]{:S(2)}) collective-permute-start(bf16[64,3072]{1,0:T(8,128)(2,1)S(1)} %get-tuple-element.141), channel_id=1, source_target_pairs={{0,2},{1,3},{2,0},{3,1},{4,6},{5,7},{6,4},{7,5},{8,10},{9,11},{10,... | collective-permute-start | bytes 1179656 | tf_op jit(solution)/shard_map/ppermute | solution.py:296
  65.7 9.4 %collective-permute-start.19 = (bf16[1536,128]{1,0:T(8,128)(2,1)S(1)}, bf16[1536,128]{1,0:T(8,128)(2,1)S(1)}, u32[]{:S(2)}, u32[]{:S(2)}) collective-permute-start(bf16[1536,128]{1,0:T(8,128)(2,1)S(1)} %collective-permute-done.17.refs_5_.refs_13_), channel_id=1, source_target_pairs={{0,8},{8,16},{16,24},{24,28},{28,20},{20,12},{12,4},{4,0},{1,9},{9... | collective-permute-start | bytes 1179656 | tf_op jit(solution)/shard_map/ppermute | solution.py:247
  66.5 12.7 %collective-permute-start.20 = (bf16[48,3072]{1,0:T(8,128)(2,1)S(1)}, bf16[48,3072]{1,0:T(8,128)(2,1)S(1)}, u32[]{:S(2)}, u32[]{:S(2)}) collective-permute-start(bf16[48,3072]{1,0:T(8,128)(2,1)S(1)} %get-tuple-element.167), channel_id=1, source_target_pairs={{0,2},{1,3},{2,0},{3,1},{4,6},{5,7},{6,4},{7,5},{8,10},{9,11},{10,... | collective-permute-start | bytes 884744 | tf_op jit(solution)/shard_map/ppermute | solution.py:296
  79.2 9.4 %collective-permute-start.22 = (bf16[256,3072]{1,0:T(8,128)(2,1)S(1)}, bf16[256,3072]{1,0:T(8,128)(2,1)S(1)}, u32[]{:S(2)}, u32[]{:S(2)}) collective-permute-start(bf16[256,3072]{1,0:T(8,128)(2,1)S(1)} %down_grad.8), channel_id=1, source_target_pairs={{0,1},{1,0},{2,3},{3,2},{4,5},{5,4},{6,7},{7,6},{8,9},{9,8},{10,11... | collective-permute-start | bytes 4718600 | tf_op jit(solution)/shard_map/ppermute | solution.py:293
  79.2 9.4 %collective-permute-start.21 = (bf16[48,3072]{1,0:T(8,128)(2,1)S(1)}, bf16[48,3072]{1,0:T(8,128)(2,1)S(1)}, u32[]{:S(2)}, u32[]{:S(2)}) collective-permute-start(bf16[48,3072]{1,0:T(8,128)(2,1)S(1)} %get-tuple-element.170), channel_id=1, source_target_pairs={{0,2},{1,3},{2,0},{3,1},{4,6},{5,7},{6,4},{7,5},{8,10},{9,11},{10,... | collective-permute-start | bytes 884744 | tf_op jit(solution)/shard_map/ppermute | solution.py:296
  88.6 5.7 %collective-permute-start.24 = (bf16[512,3072]{1,0:T(8,128)(2,1)S(1)}, bf16[512,3072]{1,0:T(8,128)(2,1)S(1)}, u32[]{:S(2)}, u32[]{:S(2)}) collective-permute-start(bf16[512,3072]{1,0:T(8,128)(2,1)S(1)} %down_grad.9), channel_id=1, source_target_pairs={{0,1},{1,0},{2,3},{3,2},{4,5},{5,4},{6,7},{7,6},{8,9},{9,8},{10,11... | collective-permute-start | bytes 9437192 | tf_op jit(solution)/shard_map/ppermute | solution.py:293
  91.8 23.9 %collective-permute-start.23 = (bf16[128,3072]{1,0:T(8,128)(2,1)S(1)}, bf16[128,3072]{1,0:T(8,128)(2,1)S(1)}, u32[]{:S(2)}, u32[]{:S(2)}) collective-permute-start(bf16[128,3072]{1,0:T(8,128)(2,1)S(1)} %get-tuple-element.175), channel_id=1, source_target_pairs={{0,2},{1,3},{2,0},{3,1},{4,6},{5,7},{6,4},{7,5},{8,10},{9,11},{10,... | collective-permute-start | bytes 2359304 | tf_op jit(solution)/shard_map/ppermute | solution.py:296
  93.4 28.4 %collective-permute-start.25 = (bf16[64,3072]{1,0:T(8,128)(2,1)S(1)}, bf16[64,3072]{1,0:T(8,128)(2,1)S(1)}, u32[]{:S(2)}, u32[]{:S(2)}) collective-permute-start(bf16[64,3072]{1,0:T(8,128)(2,1)S(1)} %get-tuple-element.177), channel_id=1, source_target_pairs={{0,2},{1,3},{2,0},{3,1},{4,6},{5,7},{6,4},{7,5},{8,10},{9,11},{10,... | collective-permute-start | bytes 1179656 | tf_op jit(solution)/shard_map/ppermute | solution.py:296
  93.9 5.5 %copy-start.1 = (bf16[4,1,640,768]{3,2,1,0:T(8,128)(2,1)S(1)}, bf16[4,1,640,768]{3,2,1,0:T(8,128)(2,1)}, u32[]{:S(2)}) copy-start(bf16[4,1,640,768]{3,2,1,0:T(8,128)(2,1)} %param.8) | copy-start | bytes 11796484
  115.7 6.0 %collective-permute-start.26 = (f32[1,4,4,128]{3,1,2,0:T(4,128)S(1)}, f32[1,4,4,128]{3,1,2,0:T(4,128)S(1)}, u32[]{:S(2)}, u32[]{:S(2)}) collective-permute-start(f32[1,4,4,128]{3,1,2,0:T(4,128)S(1)} %get-tuple-element.215), channel_id=1, source_target_pairs={{0,16},{4,20},{8,24},{12,28},{16,0},{20,4},{24,8},{28,12},{1,17},{... | collective-permute-start | bytes 24584 | tf_op jit(solution)/shard_map/ppermute | solution.py:358
  117.2 11.5 %collective-permute-start.27 = (bf16[64,3072]{1,0:T(8,128)(2,1)S(1)}, bf16[64,3072]{1,0:T(8,128)(2,1)S(1)}, u32[]{:S(2)}, u32[]{:S(2)}) collective-permute-start(bf16[64,3072]{1,0:T(8,128)(2,1)S(1)} %get-tuple-element.178), channel_id=1, source_target_pairs={{0,2},{1,3},{2,0},{3,1},{4,6},{5,7},{6,4},{7,5},{8,10},{9,11},{10,... | collective-permute-start | bytes 1179656 | tf_op jit(solution)/shard_map/ppermute | solution.py:296
  121.8 3.7 %collective-permute-start.28 = (f32[2,2,4,128]{3,1,0,2:T(2,128)S(1)}, f32[2,2,4,128]{3,1,0,2:T(2,128)S(1)}, u32[]{:S(2)}, u32[]{:S(2)}) collective-permute-start(f32[2,2,4,128]{3,1,0,2:T(2,128)S(1)} %get-tuple-element.213), channel_id=1, source_target_pairs={{0,8},{4,12},{8,0},{12,4},{16,24},{20,28},{24,16},{28,20},{1,9},{5... | collective-permute-start | bytes 24584 | tf_op jit(solution)/shard_map/ppermute | solution.py:358
  128.7 0.7 copy-start.4
  130.0 4.0 %collective-permute-start.29 = (f32[4,1,4,128]{3,2,0,1:T(4,128)}, f32[4,1,4,128]{3,2,0,1:T(4,128)}, u32[]{:S(2)}, u32[]{:S(2)}) collective-permute-start(f32[4,1,4,128]{3,2,0,1:T(4,128)} %bitcast.36), channel_id=1, source_target_pairs={{0,4},{4,0},{8,12},{12,8},{16,20},{20,16},{24,28},{28,24},{1,5},{5... | collective-permute-start | bytes 24584 | tf_op jit(solution)/shard_map/ppermute | solution.py:358
  130.5 1.0 copy-start.5
  131.5 3.2 %copy-start.8 = (s32[128,8]{0,1:T(8,128)S(1)}, s32[128,8]{0,1:T(8,128)}, u32[]{:S(2)}) copy-start(s32[128,8]{0,1:T(8,128)} %param.7) | copy-start | bytes 12292
